TPU v7x, 512 devices: a whole 4x4x16 slice. The times are simulated.
512 devices in a mesh: text: 16 (over y, x_hi, core), vis: 32 (over z, x_lo).
Axes of the slice: x: 4 (x_hi: 2, x_lo: 2; x = x_hi * 2 + x_lo), y: 4, z: 16, core: 2. Of those that a mesh axis runs over, the one named last changes fastest.
Arguments:
- text_rows: bfloat16 [512, 4096], P('text', 'vis'), may hold values from -6 to 6
- visual: bfloat16 [16384, 4096], P('vis', 'text'), may hold values from -9 to 9
- norm_gain: float32 [4096], replicated, may hold values from 0.25 to 1.75
- q_weight: bfloat16 [4096, 4096], P(None, 'vis'), may hold values from -0.09375 to 0.09375
- key_value_weight: bfloat16 [4096, 2048], P(None, 'text'), may hold values from -0.09375 to 0.09375
- q_gain: float32 [128], replicated, may hold values from 0.8 to 8
- k_gain: float32 [128], replicated, may hold values from 0.8 to 8
- out_weight: bfloat16 [4096, 4096], P('vis'), may hold values from -0.29882812 to 0.29882812
- attn_gate: float32 [1], replicated, may hold values from 0.6 to 1.5
Outputs:
- gated: bfloat16 [512, 4096], P('text', 'vis')
All inputs are finite; a program needn't handle non-finite values.
Results may differ from a plain program's by a relative error of at most 0.007.
The roundings to bfloat16 on the way count: a program that leaves them out, or rounds other values in their place, can miss the bound.
Values may be sent and summed in bfloat16 or wider, within the bound.
A program may use at most 64 MiB of HBM per device.

v0:
```python
import jax
import jax.numpy as jnp
from jax import lax
from jax.sharding import PartitionSpec as P

QUERY_HEAD_COUNT = 32
KEY_VALUE_HEADS = 8
HEAD_SIZE = 128


def combined_all(shard, axis, combine):
    everything = jax.tree.map(lambda part: lax.all_gather(part, axis), shard)
    leading = jax.tree.map(lambda part: part[0], everything)

    def step(k, so_far):
        return combine(so_far, jax.tree.map(lambda part: part[k], everything))

    return lax.fori_loop(1, lax.axis_size(axis), step, leading)


def head_norm(heads, gain):
    mean_square = jnp.mean(heads * heads, axis=-1, keepdims=True)
    return heads * lax.rsqrt(mean_square + 1e-05) * gain


def on_device(
    text_rows, visual, norm_gain, q_weight, key_value_weight, q_gain, k_gain, out_weight, attn_gate
):
    count_of_rows = text_rows.shape[0]
    q_columns = q_weight.shape[1]
    local_heads = q_columns // HEAD_SIZE
    scaled = (
        lax.all_gather(text_rows, "vis", axis=1, tiled=True).astype(jnp.float32) * norm_gain
    ).astype(jnp.bfloat16)
    weight_rows = q_weight
    query_raw = jnp.dot(scaled, weight_rows, preferred_element_type=jnp.float32)
    query_local = head_norm(query_raw.reshape(count_of_rows, local_heads, HEAD_SIZE), q_gain)
    query_local = query_local.astype(jnp.bfloat16).reshape(count_of_rows, q_columns)
    query_rows = lax.all_gather(query_local, "vis", axis=1, tiled=True)
    count_of_tokens = visual.shape[0]
    weight_rows = key_value_weight
    kv_local = jnp.dot(
        lax.all_gather(visual, "text", axis=1, tiled=True),
        weight_rows,
        preferred_element_type=jnp.float32,
    )
    key_value_rows = lax.all_gather(kv_local.astype(jnp.bfloat16), "text", axis=1, tiled=True)
    unscaled_keys = (
        key_value_rows[:, : KEY_VALUE_HEADS * HEAD_SIZE]
        .astype(jnp.float32)
        .reshape(count_of_tokens, KEY_VALUE_HEADS, HEAD_SIZE)
    )
    head_keys = head_norm(unscaled_keys, k_gain).astype(jnp.bfloat16)
    head_values = key_value_rows[:, KEY_VALUE_HEADS * HEAD_SIZE :].reshape(
        count_of_tokens, KEY_VALUE_HEADS, HEAD_SIZE
    )
    query_group_width = QUERY_HEAD_COUNT // KEY_VALUE_HEADS
    grouped_queries = query_rows.reshape(
        count_of_rows, KEY_VALUE_HEADS, query_group_width, HEAD_SIZE
    )
    scale = 1.0 / jnp.sqrt(jnp.float32(HEAD_SIZE))
    scores = (
        jnp.einsum("rhgd,khd->rhgk", grouped_queries, head_keys, preferred_element_type=jnp.float32)
        * scale
    )
    row_peak = jnp.max(scores, axis=-1)
    weights = jnp.exp(scores - row_peak[..., None])
    row_total = jnp.sum(weights, axis=-1)
    partial_value = jnp.einsum(
        "rhgk,khd->rhgd",
        weights.astype(jnp.bfloat16),
        head_values,
        preferred_element_type=jnp.float32,
    )
    partial_value = partial_value.reshape(count_of_rows, QUERY_HEAD_COUNT * HEAD_SIZE)
    row_peak = row_peak.reshape(count_of_rows, QUERY_HEAD_COUNT)
    row_total = row_total.reshape(count_of_rows, QUERY_HEAD_COUNT)

    def combine_parts(first, second):
        first_out, first_peak, first_total = first
        second_out, second_peak, second_total = second
        top_score = jnp.maximum(first_peak, second_peak)
        first_factor = jnp.exp(first_peak - top_score)
        second_factor = jnp.exp(second_peak - top_score)
        heads_out = (
            first_out.reshape(count_of_rows, QUERY_HEAD_COUNT, HEAD_SIZE) * first_factor[..., None]
            + second_out.reshape(count_of_rows, QUERY_HEAD_COUNT, HEAD_SIZE)
            * second_factor[..., None]
        )
        return (
            heads_out.reshape(count_of_rows, QUERY_HEAD_COUNT * HEAD_SIZE),
            top_score,
            first_total * first_factor + second_total * second_factor,
        )

    merged, top_score, denominator = combined_all(
        (partial_value, row_peak, row_total), "vis", combine_parts
    )
    first_head = lax.axis_index("vis") * local_heads
    numerator = lax.dynamic_slice_in_dim(
        merged.reshape(count_of_rows, QUERY_HEAD_COUNT, HEAD_SIZE), first_head, local_heads, 1
    )
    denominator = lax.dynamic_slice_in_dim(denominator, first_head, local_heads, 1)
    attended = (
        (numerator / denominator[..., None]).astype(jnp.bfloat16).reshape(count_of_rows, q_columns)
    )
    out_terms = jnp.dot(attended, out_weight, preferred_element_type=jnp.float32)
    summed = lax.psum_scatter(out_terms, "vis", scatter_dimension=1, tiled=True)
    return (jnp.tanh(attn_gate[0]) * summed).astype(jnp.bfloat16)


def solution(mesh):
    placed = (
        P("text", "vis"),
        P("vis", "text"),
        P(),
        P(None, "vis"),
        P(None, "text"),
        P(),
        P(),
        P("vis", None),
        P(),
    )
    return jax.shard_map(
        on_device, mesh=mesh, in_specs=placed, out_specs=P("text", "vis"), check_vma=False
    )
```

profile of v0, /device:TPU:24, one launch (start us, length us, event | category | flops | bytes accessed | tf_op | source)
XLA Modules:
  0.0 822.4 jit_solution(9599685915993373545)
XLA Ops:
  7.3 77.6 %all-gather.4.cloned.1.call-done = bf16[512,4096]{1,0:T(8,128)(2,1)} async-done(((bf16[512,256]{1,0:T(8,128)(2,1)}), bf16[512,4096]{1,0:T(8,128)(2,1)}) %all-gather.4.cloned.1.call-update) | async-done | bytes 4194320 | tf_op jit(solution)/shard_map/all_gather | solution.py:43
  84.9 4.4 convolution_convert_fusion
  89.4 64.2 %all_gather.23 = bf16[32,4096]{1,0:T(8,128)(2,1)S(1)} all-gather(bf16[32,128]{1,0:T(8,128)(2,1)S(1)} %copy-done.4), channel_id=1, replica_groups=mesh['text'=16,'vis'=32] {'vis'}, dimensions={1}, use_global_device_ids=true | all-gather | bytes 270336 | tf_op jit(solution)/shard_map/all_gather | solution.py:33
  154.1 59.7 %all_gather.24 = bf16[32,4096]{1,0:T(8,128)(2,1)S(1)} all-gather(bf16[32,128]{1,0:T(8,128)(2,1)S(1)} %multiply_convert_fusion.4), channel_id=1, replica_groups=mesh['text'=16,'vis'=32] {'vis'}, dimensions={1}, use_global_device_ids=true | all-gather | bytes 270336 | tf_op jit(solution)/shard_map/all_gather | solution.py:39
  213.8 0.9 reshape.85
  214.7 2.9 slice_bitcast_fusion
  219.0 1.5 copy.53
  222.6 1.1 copy.41
  223.8 2.1 all_gather_reshape.9
  226.6 74.6 %all_gather.27 = f32[32,32,32]{2,1,0:T(8,128)S(1)} all-gather(f32[1,32,32]{2,1,0:T(8,128)S(1)} %copy.43), channel_id=1, replica_groups=mesh['text'=16,'vis'=32] {'vis'}, dimensions={0}, use_global_device_ids=true | all-gather | bytes 135168 | tf_op jit(solution)/shard_map/all_gather | solution.py:12
  301.2 72.8 %all_gather.26 = f32[32,32,32]{2,1,0:T(8,128)S(1)} all-gather(f32[1,32,32]{2,1,0:T(8,128)S(1)} %copy.42), channel_id=1, replica_groups=mesh['text'=16,'vis'=32] {'vis'}, dimensions={0}, use_global_device_ids=true | all-gather | bytes 135168 | tf_op jit(solution)/shard_map/all_gather | solution.py:12
  374.0 233.7 %all-gather.8.cloned.1.call-done = f32[32,32,4096]{2,1,0:T(8,128)} async-done(((f32[1,32,4096]{2,1,0:T(8,128)}), f32[32,32,4096]{2,1,0:T(8,128)}) %all-gather.8.cloned.1.call-update) | async-done | bytes 16777232 | tf_op jit(solution)/shard_map/all_gather | solution.py:12
  607.7 1.1 slice_bitcast_fusion.1
  608.7 68.8 %while.19 = (s32[]{:T(128)}, f32[32,4096]{1,0:T(8,128)S(1)}, f32[32,32]{1,0:T(8,128)S(1)}, f32[32,32]{1,0:T(8,128)S(1)}, f32[32,32,32]{2,1,0:T(8,128)S(1)}, /*in...) while((s32[]{:T(128)}, f32[32,4096]{1,0:T(8,128)S(1)}, ...), condition=%wide.region_5.0_spmd, body=%wide.region_4.0_spmd.sunk | while | flops 399365 | bytes 3711127 | solution.py:18
  609.2 1.8 fusion.28
  611.4 1.8 fusion.28
  613.6 1.8 fusion.28
  615.8 1.8 fusion.28
  618.1 1.8 fusion.28
  620.3 1.8 fusion.28
  622.5 1.8 fusion.28
  624.7 1.8 fusion.28
  626.9 1.8 fusion.28
  629.2 1.8 fusion.28
  631.4 1.8 fusion.28
  633.6 1.8 fusion.28
  635.8 1.8 fusion.28
  638.0 1.8 fusion.28
  640.3 1.8 fusion.28
  642.5 1.8 fusion.28
  644.7 1.8 fusion.28
  646.9 1.8 fusion.28
  649.1 1.8 fusion.28
  651.4 1.8 fusion.28
  653.6 1.8 fusion.28
  655.8 1.8 fusion.28
  658.0 1.8 fusion.28
  660.2 1.8 fusion.28
  662.4 1.8 fusion.28
  664.7 1.8 fusion.28
  666.9 1.8 fusion.28
  669.1 1.8 fusion.28
  671.3 1.8 fusion.28
  673.5 1.8 fusion.28
  675.8 1.8 fusion.28
  678.0 1.1 fusion.16
  679.7 134.8 %reduce-scatter.2.cloned.1.call-done = f32[32,128]{1,0:T(8,128)} async-done(((f32[32,4096]{1,0:T(8,128)}), f32[32,128]{1,0:T(8,128)}) %reduce-scatter.2.cloned.1.call-update) | async-done | bytes 16400 | tf_op jit(solution)/shard_map/reduce_scatter | solution.py:108
  814.6 1.3 multiply_convert_fusion.3
  (135 shorter events, 18.6 us)
Async XLA Ops:
  6.5 671.4 %copy-start = (bf16[128,4096]{1,0:T(8,128)(2,1)S(1)}, bf16[128,4096]{1,0:T(8,128)(2,1)}, u32[]{:S(2)}) copy-start(bf16[128,4096]{1,0:T(8,128)(2,1)} %param.18) | copy-start | bytes 3145732
  6.5 78.4 %all-gather.4.cloned.1.call-start = ((), (), s32[]{:S(2)}) async-start(), calls=%async_computation.1 | async-start | bytes 4456448 | tf_op jit(solution)/shard_map/all_gather | solution.py:43
  7.3 82.1 %copy-start.4 = (bf16[32,128]{1,0:T(8,128)(2,1)S(1)}, bf16[32,128]{1,0:T(8,128)(2,1)}, u32[]{:S(2)}) copy-start(bf16[32,128]{1,0:T(8,128)(2,1)} %param.11) | copy-start | bytes 24580
  7.3 146.3 %copy-start.1 = (bf16[4096,128]{1,0:T(8,128)(2,1)S(1)}, bf16[4096,128]{1,0:T(8,128)(2,1)}, u32[]{:S(2)}) copy-start(bf16[4096,128]{1,0:T(8,128)(2,1)} %param.14) | copy-start | bytes 3145732
  7.3 146.3 %copy-start.3 = (f32[4096]{0:T(1024)S(1)}, f32[4096]{0:T(1024)}, u32[]{:S(2)}) copy-start(f32[4096]{0:T(1024)} %param.13) | copy-start | bytes 49156
  7.3 146.7 %copy-start.6 = (f32[128]{0:T(128)S(1)}, f32[128]{0:T(128)}, u32[]{:S(2)}) copy-start(f32[128]{0:T(128)} %param.16) | copy-start | bytes 1540
  7.3 207.4 %all-gather.6.cloned.1.call-start = ((), (), s32[]{:S(2)}) async-start(), calls=%async_computation.2 | async-start | bytes 2228224 | tf_op jit(solution)/shard_map/all_gather | solution.py:47
  89.3 518.3 %all-gather.8.cloned.1.call-start = ((), (), s32[]{:S(2)}) async-start(), calls=%async_computation.3 | async-start | bytes 17301504 | tf_op jit(solution)/shard_map/all_gather | solution.py:12
  218.1 2.4 copy-start.5
  220.5 1.0 copy-start.2
  225.8 588.7 %reduce-scatter.2.cloned.1.call-start = ((), (), s32[]{:S(2)}) async-start(), calls=%async_computation.4 | async-start | bytes 540672 | tf_op jit(solution)/shard_map/reduce_scatter | solution.py:108
Sparse Core Ops, SparseCore 0:
  10.6 74.3 all-gather.3
  89.5 60.9 all-gather.5
  226.0 381.6 all-gather.7
  679.2 135.3 reduce-scatter.1
where the time goes:
time: 825 us; the launch traced here: 822 us
  waiting for transfers between devices  447 us (54%)
  blocking collectives  271 us (33%)
  other arithmetic  62.1 us (8%)
  local copies, waits for them, and re-layouts  19.7 us (2%)
  between operations  14 us (2%)
    all_gather x1, waiting for transfers between devices, combined_all(): everything = jax.tree.map(lambda part: lax.all_gather(part, axis), shard)  234 us
    all_gather x2, blocking collectives, combined_all(): everything = jax.tree.map(lambda part: lax.all_gather(part, axis), shard)  147 us
    reduce_scatter x1, waiting for transfers between devices, on_device(): summed = lax.psum_scatter(out_terms, 'vis', scatter_dimension=1, tiled=True)  135 us
    all_gather x1, waiting for transfers between devices, on_device(): lax.all_gather(visual, 'text', axis=1, tiled=True)  77.6 us
    all_gather x1, blocking collectives, on_device(): lax.all_gather(text_rows, 'vis', axis=1, tiled=True).astype(jnp.float32)  64.2 us
    all_gather x1, blocking collectives, on_device(): query_rows = lax.all_gather(query_local, 'vis', axis=1, tiled=True)  59.7 us
    add x31, other arithmetic, combine_parts(): first_out.reshape(count_of_rows, QUERY_HEAD_COUNT, HEAD_SIZE)  54.8 us
  transfers between devices with their start and end apart: 4, of which 3 were waited for; matrix products, arithmetic and copies ran while one was open for 0% of the time, Pallas kernels for 0%

commit v1 on v0

v1 whole, which is shorter than its diff:
```python
import jax
import jax.numpy as jnp
from jax import lax
from jax.experimental import pallas as pl
from jax.experimental.pallas import tpu as pltpu
from jax.sharding import PartitionSpec as P

HEAD = 128
EPS = 1e-05
SCALE_LOG2 = (HEAD ** -0.5) * 1.4426950408889634
MESH = pl.DeviceIdType.MESH
BF16 = jnp.bfloat16
F32 = jnp.float32


def rcopy(src, dst, send, recv, t, v):
    return pltpu.make_async_remote_copy(
        src_ref=src, dst_ref=dst, send_sem=send, recv_sem=recv, device_id=(t, v), device_id_type=MESH
    )


def head_norm(heads, gain):
    mean_square = jnp.mean(heads * heads, axis=-1, keepdims=True)
    return heads * lax.rsqrt(mean_square + EPS) * gain


def column_tile(m, l):
    lane = lax.broadcasted_iota(jnp.int32, (8, 128), 1)
    tile = jnp.zeros((8, 128), F32)
    for k in range(32):
        tile = jnp.where(lane == k, m[8 * k : 8 * k + 8], tile)
        tile = jnp.where(lane == 32 + k, l[8 * k : 8 * k + 8], tile)
    return tile


def kernel(
    text_ref, vis_ref, gain_ref, wq_hbm, wkv_hbm, qg_ref, kg_ref, wo_hbm, gate_ref,
    out_ref,
    text_s, text_all, wq, wk, vb, q_loc, qbuf, kvst, kvb,
    o_send, t_send, o_own, t_own, o_recv, t_recv, o2, t2, d_all, t_all,
    att, att_all, wo2, r_send, r_recv,
    loc, vsend, vrecv, wsend, wrecv, tsend, trecv, txsend, txrecv, c1send, c1recv,
    qsend, qfsend, qrecv, wosend, worecv, kvsend, kvrecv, osend, orecv, ssend, srecv,
    dsend, drecv, t2send, t2recv, asend, arecv, rsend, rrecv,
):
    t = lax.axis_index("text")
    v = lax.axis_index("vis")
    z = v // 2
    xl = v % 2
    c = t % 2
    half = t // 8
    g = t % 8
    vx = 2 * z + 1 - xl
    sib = t + 1 - 2 * c
    xh = (t // 2) % 2
    base = (t // 4) * 4
    xp = base + (1 - xh) * 2 + c
    xps = base + (1 - xh) * 2 + 1 - c
    up = (t + 4) % 16
    dn = (t + 12) % 16
    far = (t + 8) % 16
    col = t - c
    far_sib = (sib + 8) % 16
    t1 = half * 8 + v // 4
    v1 = g * 4 + v % 4
    v2 = g * 4 + (v % 4) + 1 - 2 * (v % 2)
    owner = g == v // 4
    j_own = v % 4

    def at_z(zz):
        return 2 * zz + xl

    def ring(i):
        return lax.rem(z + 8 + jnp.where(i % 2 == 0, -(i // 2), (i + 1) // 2), 16)

    def each_z(body):
        def step(i, carry):
            body(ring(i))
            return carry

        lax.fori_loop(0, 15, step, 0)

    own_tokens = pltpu.make_async_copy(vis_ref.at[pl.ds(c * 256, 256), :], vb.at[t], loc.at[0])
    own_wq = pltpu.make_async_copy(wq_hbm, wq, loc.at[1])
    own_wk = pltpu.make_async_copy(wkv_hbm, wk.at[:, pl.ds(pl.multiple_of(c * 128, 128), 128)], loc.at[2])
    own_tokens.start()
    own_wk.start()
    own_wq.start()
    gain = gain_ref[:, pl.ds(pl.multiple_of(v * 128, 128), 128)]
    text_s[...] = (text_ref[...].astype(F32) * gain).astype(BF16)
    my_cols = pl.ds(pl.multiple_of(z * 128, 128), 128)
    text_all[xl, :, my_cols] = text_s[...]

    barrier = pltpu.get_barrier_semaphore()

    def greet(tt, vv):
        pl.semaphore_signal(barrier, inc=1, device_id=(tt, vv), device_id_type=MESH)

    each_z(lambda zz: greet(t, at_z(zz)))
    greet(t, vx)
    for other in (sib, xp, up, dn, far, far_sib):
        greet(other, v)
    greet(t1, v2)

    @pl.when(owner)
    def _():
        def step(i, carry):
            greet(half * 8 + lax.rem(g + i, 8), v)
            return carry

        lax.fori_loop(1, 8, step, 0)

    @pl.when(jnp.logical_not(owner))
    def _():
        greet(t1, v)
        greet(t1, v1)

    pl.semaphore_wait(barrier, 15 + 1 + 6 + 1 + jnp.where(owner, 7, 2))

    rows_here = pl.ds(c * 256, 256)
    rows_sib = pl.ds((1 - c) * 256, 256)
    to_sib = rcopy(vis_ref.at[rows_sib, :], vb.at[t], vsend.at[0], vrecv.at[t], sib, v)
    to_sib.start()

    def push_text(zz):
        rcopy(text_s, text_all.at[xl, :, my_cols], tsend, trecv, t, at_z(zz)).start()

    each_z(push_text)
    sends = [to_sib]

    def send_block(f, target, src=None):
        copy = rcopy(
            vb.at[f] if src is None else src, vb.at[f], vsend.at[len(sends)], vrecv.at[f], target, v
        )
        copy.start()
        sends.append(copy)

    for target in (up, dn, xp):
        send_block(t, target, vis_ref.at[rows_here, :])
    w_out = rcopy(
        wkv_hbm, wk.at[:, pl.ds(pl.multiple_of(c * 128, 128), 128)], wsend, wrecv, sib, v
    )
    w_out.start()

    def got(f):
        rcopy(vb.at[f], vb.at[f], vsend.at[0], vrecv.at[f], sib, v).wait_recv()

    acc = jnp.zeros((256, 256), F32)

    def add(acc, f):
        weights = wk[pl.ds(pl.multiple_of(f * 256, 256), 256), :]
        return acc + jnp.dot(vb[f], weights, preferred_element_type=F32)

    got(sib)
    for target in (up, dn, xp):
        send_block(sib, target)

    z_bytes = text_all.at[0, :, pl.ds(0, 15 * 128)]
    rcopy(z_bytes, z_bytes, tsend, trecv, t, vx).wait_recv()
    text_x = rcopy(text_all.at[xl], text_all.at[xl], txsend, txrecv, t, vx)
    text_x.start()

    got(xp)
    for target in (up, dn):
        send_block(xp, target)
    got(xps)
    for target in (up, dn):
        send_block(xps, target)

    up0, up1 = (col + 4) % 16, (col + 5) % 16
    dn0, dn1 = (col + 12) % 16, (col + 13) % 16
    pcol = base + (1 - xh) * 2
    pup0, pup1 = (pcol + 4) % 16, (pcol + 5) % 16
    pdn0, pdn1 = (pcol + 12) % 16, (pcol + 13) % 16
    got(dn0)
    send_block(dn0, up)
    got(up1)
    send_block(up1, dn)

    text_other = text_all.at[1 - xl]
    rcopy(text_other, text_other, txsend, txrecv, t, vx).wait_recv()
    own_wq.wait()
    q = jnp.zeros((32, 128), F32)
    for k in range(16):
        lhs = jnp.concatenate(
            [text_all[0, :, k * 128 : k * 128 + 128], text_all[1, :, k * 128 : k * 128 + 128]], axis=1
        )
        q = q + jnp.dot(lhs, wq[k * 256 : k * 256 + 256, :], preferred_element_type=F32)
    q_loc[...] = head_norm(q, qg_ref[...]).astype(BF16)
    my_rows = pl.ds(pl.multiple_of(g * 32, 32), 32)
    c1 = rcopy(q_loc, qbuf.at[j_own, my_rows, :], c1send, c1recv.at[g], t1, v)

    @pl.when(jnp.logical_not(owner))
    def _():
        c1.start()

    got(pdn0)
    send_block(pdn0, up)
    got(pup1)
    send_block(pup1, dn)

    def wo_step(zz, carry):
        src_own = wo_hbm.at[:, pl.ds(pl.multiple_of((2 * zz + xl) * 128, 128), 128)]
        src_out = wo_hbm.at[:, pl.ds(pl.multiple_of((2 * zz + 1 - xl) * 128, 128), 128)]
        dst = wo2.at[xl, :, pl.ds(pl.multiple_of(zz * 128, 128), 128)]
        pltpu.make_async_copy(src_own, dst, loc.at[3]).start()
        rcopy(src_out, dst, wosend, worecv, t, vx).start()
        return carry

    q_own = qbuf.at[j_own]

    def push_q(zz):
        rcopy(q_own, q_own, qsend, qrecv.at[j_own], t, at_z(zz)).start()

    @pl.when(owner)
    def _():
        qbuf[j_own, my_rows, :] = q_loc[...]

        def step(i, carry):
            s = lax.rem(g + i, 8)
            part = qbuf.at[j_own, pl.ds(pl.multiple_of(s * 32, 32), 32), :]
            rcopy(part, part, c1send, c1recv.at[s], t1, v).wait_recv()
            return carry

        lax.fori_loop(1, 8, step, 0)
        each_z(push_q)

    lax.fori_loop(0, 16, wo_step, 0)

    own_tokens.wait()
    own_wk.wait()
    wk_other = wk.at[:, pl.ds(pl.multiple_of((1 - c) * 128, 128), 128)]
    rcopy(wk_other, wk_other, wsend, wrecv, sib, v).wait_recv()
    acc = add(acc, t)
    acc = add(acc, sib)
    acc = add(acc, xp)
    acc = add(acc, xps)
    acc = add(acc, dn0)
    acc = add(acc, up1)
    acc = add(acc, pdn0)
    acc = add(acc, pup1)
    for f in (dn1, up0, pdn1, pup0):
        got(f)
        acc = add(acc, f)

    for jj in range(2):
        j = 2 * jj + xl

        @pl.when(v != 4 * g + j)
        def _():
            rcopy(qbuf.at[j], qbuf.at[j], qsend, qrecv.at[j], t, vx).wait_recv()

        rcopy(qbuf.at[j], qbuf.at[j], qfsend.at[jj], qrecv.at[j], t, vx).start()

    far0, far1 = (col + 8) % 16, (col + 9) % 16
    pfar0, pfar1 = (pcol + 8) % 16, (pcol + 9) % 16
    for f in (far0, far1, pfar0, pfar1):
        got(f)
        acc = add(acc, f)

    kv = acc.astype(BF16)
    raw = kv.astype(F32)
    for h in range(2):
        part = raw[:, h * 128 : h * 128 + 128]
        normed = head_norm(part, kg_ref[...])
        kvst[h] = jnp.where(half == 0, normed, part).astype(BF16)
    my_half = pl.ds(pl.multiple_of(c * 256, 256), 256)
    other_half = pl.ds(pl.multiple_of((1 - c) * 256, 256), 256)
    kv_sib = rcopy(kvst.at[1 - c], kvb.at[half, my_half, :], kvsend.at[0], kvrecv.at[0], sib, v)
    kv_far = rcopy(kvst.at[c], kvb.at[half, my_half, :], kvsend.at[1], kvrecv.at[1], far, v)
    kv_far_sib = rcopy(kvst.at[1 - c], kvb.at[half, my_half, :], kvsend.at[2], kvrecv.at[2], far_sib, v)
    kv_far.start()
    kv_far_sib.start()
    kv_sib.start()
    kvb[half, my_half, :] = kvst[c]

    for jj in range(2):
        j = 2 * jj + 1 - xl
        rcopy(qbuf.at[j], qbuf.at[j], qsend, qrecv.at[j], t, vx).wait_recv()
    rcopy(kvst.at[0], kvb.at[half, other_half, :], kvsend.at[0], kvrecv.at[0], sib, v).wait_recv()
    rcopy(kvst.at[0], kvb.at[1 - half, my_half, :], kvsend.at[1], kvrecv.at[1], far, v).wait_recv()
    rcopy(kvst.at[0], kvb.at[1 - half, other_half, :], kvsend.at[2], kvrecv.at[2], far, v).wait_recv()

    def attend(j):
        scores = lax.dot_general(
            qbuf[j], kvb[0], (((1,), (1,)), ((), ())), preferred_element_type=F32
        )
        peak = jnp.max(scores, axis=-1, keepdims=True)
        probs = jnp.exp2((scores - peak) * SCALE_LOG2)
        total = jnp.sum(probs, axis=-1, keepdims=True)
        partial = jnp.dot(probs.astype(BF16), kvb[1], preferred_element_type=F32)
        return partial, column_tile(peak * SCALE_LOG2, total)

    o_out = []
    for jj in range(2):
        partial, tile = attend(2 * jj + 1 - xl)
        o_send[jj] = partial.astype(BF16)
        t_send[jj] = tile
        copy = rcopy(o_send.at[jj], o_recv.at[jj], osend.at[jj], orecv.at[jj], t, vx)
        copy.start()
        o_out.append(copy)
        copy = rcopy(t_send.at[jj], t_recv.at[jj], ssend.at[jj], srecv.at[jj], t, vx)
        copy.start()
        o_out.append(copy)
    for jj in range(2):
        partial, tile = attend(2 * jj + xl)
        o_own[jj] = partial
        t_own[jj] = tile

    for jj in range(2):
        o_out[2 * jj].wait_recv()
        o_out[2 * jj + 1].wait_recv()
        mine, theirs = t_own[jj], t_recv[jj]
        top = jnp.maximum(mine, theirs)
        a, b = jnp.exp2(mine - top), jnp.exp2(theirs - top)
        lane = lax.broadcasted_iota(jnp.int32, (8, 128), 1)
        a = jnp.where(lane < 32, a, 0.0)
        b = jnp.where(lane < 32, b, 0.0)
        total = pltpu.roll(a, 32, 1) * mine + pltpu.roll(b, 32, 1) * theirs
        tile = jnp.where(lane < 32, top, total)
        for k in range(32):
            rows = slice(8 * k, 8 * k + 8)
            o_own[jj, rows, :] = (
                o_own[jj, rows, :] * a[:, k : k + 1]
                + o_recv[jj, rows, :].astype(F32) * b[:, k : k + 1]
            )
        o2[jj] = o_own[jj].astype(BF16)
        for rb in range(8):
            t2[jj, rb] = tile if rb == 0 else pltpu.roll(tile, 128 - 4 * rb, 1)

    def push_partial(zz):
        rows = pl.ds(pl.multiple_of((zz // 2) * 32, 32), 32)
        rcopy(o2.at[zz % 2, rows, :], d_all.at[z], dsend, drecv, t, at_z(zz)).start()
        rcopy(t2.at[zz % 2, zz // 2], t_all.at[z], t2send, t2recv, t, at_z(zz)).start()

    each_z(push_partial)
    d_all[z] = o2[z % 2, pl.ds(pl.multiple_of((z // 2) * 32, 32), 32), :]
    t_all[z] = t2[z % 2, z // 2]
    d15, t15 = d_all.at[pl.ds(0, 15)], t_all.at[pl.ds(0, 15)]
    rcopy(t15, t15, t2send, t2recv, t, vx).wait_recv()
    rcopy(d15, d15, dsend, drecv, t, vx).wait_recv()
    lane = lax.broadcasted_iota(jnp.int32, (8, 128), 1)
    top = t_all[0]
    for s in range(1, 16):
        top = jnp.maximum(top, t_all[s])
    den = jnp.zeros((8, 128), F32)
    num = [jnp.zeros((8, 128), F32) for _ in range(4)]
    for s in range(16):
        tile = t_all[s]
        w = jnp.where(lane < 4, jnp.exp2(tile - top), 0.0)
        den = den + w * pltpu.roll(tile, 96, 1)
        block = d_all[s].astype(F32)
        for k in range(4):
            num[k] = num[k] + block[8 * k : 8 * k + 8] * w[:, k : k + 1]
    attended = jnp.concatenate([num[k] / den[:, k : k + 1] for k in range(4)], axis=0)
    att[...] = attended.astype(BF16)

    a1 = rcopy(att, att_all.at[xl], asend.at[0], arecv.at[xl], t1, v1)
    a2 = rcopy(att, att_all.at[xl], asend.at[1], arecv.at[xl], t1, v2)
    a2.start()

    @pl.when(jnp.logical_not(owner))
    def _():
        a1.start()
        a1.wait_recv()

    @pl.when(owner)
    def _():
        att_all[xl] = att[...]

    a_other = att_all.at[1 - xl]
    rcopy(a_other, a_other, asend.at[1], arecv.at[1 - xl], t1, v2).wait_recv()

    pltpu.make_async_copy(wo2.at[xl], wo2.at[xl], loc.at[3]).wait()
    rcopy(wo2.at[1 - xl], wo2.at[1 - xl], wosend, worecv, t, vx).wait_recv()
    for n in range(4):
        cols = slice(n * 512, n * 512 + 512)
        terms = jnp.dot(att_all[0], wo2[0, :, cols], preferred_element_type=F32) + jnp.dot(
            att_all[1], wo2[1, :, cols], preferred_element_type=F32
        )
        for k in range(4):
            r_send[4 * n + k] = terms[:, k * 128 : k * 128 + 128].astype(BF16)

    def push_out(zz):
        rcopy(r_send.at[zz], r_recv.at[z], rsend, rrecv, t, at_z(zz)).start()

    each_z(push_out)
    r_recv[z] = r_send[z]
    r15 = r_recv.at[pl.ds(0, 15)]
    rcopy(r15, r15, rsend, rrecv, t, vx).wait_recv()
    summed = r_recv[0].astype(F32)
    for s in range(1, 16):
        summed = summed + r_recv[s].astype(F32)
    out_ref[...] = (jnp.tanh(jnp.full((32, 128), gate_ref[0], F32)) * summed).astype(BF16)

    for copy in sends:
        copy.wait_send()
    w_out.wait_send()
    rcopy(z_bytes, z_bytes, tsend, trecv, t, vx).wait_send()
    text_x.wait_send()

    @pl.when(jnp.logical_not(owner))
    def _():
        c1.wait_send()
        a1.wait_send()

    @pl.when(owner)
    def _():
        def step(i, carry):
            rcopy(q_own, q_own, qsend, qrecv.at[j_own], t, vx).wait_send()
            return carry

        lax.fori_loop(0, 15, step, 0)

    for jj in range(2):
        rcopy(qbuf.at[0], qbuf.at[0], qfsend.at[jj], qrecv.at[0], t, vx).wait_send()
    rcopy(wo2.at[xl], wo2.at[xl], wosend, worecv, t, vx).wait_send()
    for copy in (kv_sib, kv_far, kv_far_sib, a2, *o_out):
        copy.wait_send()
    rcopy(d15, d15, dsend, drecv, t, vx).wait_send()
    rcopy(t15, t15, t2send, t2recv, t, vx).wait_send()
    rcopy(r15, r15, rsend, rrecv, t, vx).wait_send()


def on_device(
    text_rows, visual, norm_gain, q_weight, key_value_weight, q_gain, k_gain, out_weight, attn_gate
):
    vmem = pl.BlockSpec(memory_space=pltpu.VMEM)
    hbm = pl.BlockSpec(memory_space=pl.ANY)
    smem = pl.BlockSpec(memory_space=pltpu.SMEM)
    dma = pltpu.SemaphoreType.DMA
    one = dma(())
    buffers = [
        pltpu.VMEM(shape, dtype)
        for shape, dtype in (
            ((32, 128), BF16),
            ((2, 32, 2048), BF16),
            ((4096, 128), BF16),
            ((4096, 256), BF16),
            ((16, 256, 256), BF16),
            ((32, 128), BF16),
            ((4, 256, 128), BF16),
            ((2, 256, 128), BF16),
            ((2, 512, 128), BF16),
            ((2, 256, 128), BF16),
            ((2, 8, 128), F32),
            ((2, 256, 128), F32),
            ((2, 8, 128), F32),
            ((2, 256, 128), BF16),
            ((2, 8, 128), F32),
            ((2, 256, 128), BF16),
            ((2, 8, 8, 128), F32),
            ((16, 32, 128), BF16),
            ((16, 8, 128), F32),
            ((32, 128), BF16),
            ((2, 32, 128), BF16),
            ((2, 128, 2048), BF16),
            ((16, 32, 128), BF16),
            ((16, 32, 128), BF16),
        )
    ]
    semaphores = [
        dma((4,)),
        dma((15,)), dma((16,)),
        one, one,
        one, one, one, one,
        one, dma((8,)),
        one, dma((2,)), dma((4,)),
        one, one,
        dma((3,)), dma((3,)),
        dma((2,)), dma((2,)), dma((2,)), dma((2,)),
        one, one, one, one,
        dma((2,)), dma((2,)),
        one, one,
    ]
    return pl.pallas_call(
        kernel,
        out_shape=jax.ShapeDtypeStruct((32, 128), BF16),
        in_specs=[vmem, hbm, vmem, hbm, hbm, vmem, vmem, hbm, smem],
        out_specs=vmem,
        scratch_shapes=buffers + semaphores,
        compiler_params=pltpu.CompilerParams(
            collective_id=0, has_side_effects=True, vmem_limit_bytes=48 * 1024 * 1024
        ),
    )(
        text_rows, visual, norm_gain.reshape(1, -1), q_weight, key_value_weight,
        q_gain.reshape(1, -1), k_gain.reshape(1, -1), out_weight, attn_gate,
    )


def solution(mesh):
    placed = (
        P("text", "vis"),
        P("vis", "text"),
        P(),
        P(None, "vis"),
        P(None, "text"),
        P(),
        P(),
        P("vis", None),
        P(),
    )
    return jax.shard_map(
        on_device, mesh=mesh, in_specs=placed, out_specs=P("text", "vis"), check_vma=False
    )
```

time: 825 us -> 102 us (0.12)
  the two profiles are of different devices: /device:TPU:24 before, /device:TPU:8 now
where the time goes in v1:
time: 102 us
  Pallas kernels  93.9 us (92%)
  local copies, waits for them, and re-layouts  7.29 us (7%)
    pallas_call x1, Pallas kernels, on_device(): pl.pallas_call(kernel, out_shape=jax.ShapeDtypeStruct((32, 128), BF16), i...  93.9 us
    unnamed x17, local copies, waits for them, and re-layouts  7.29 us

profile of v1, /device:TPU:8, one launch (start us, length us, event | category | flops | bytes accessed | tf_op | source)
XLA Modules:
  0.0 101.9 jit_solution(2889043857718479296)
XLA Ops:
  0.7 0.0 copy-start.6
  0.7 0.0 copy-start.7
  0.7 0.6 copy-done.6
  1.3 0.0 copy-done.7
  1.3 0.0 copy-start
  1.3 1.2 %copy-done = bf16[4096,128]{1,0:T(8,128)(2,1)S(1)} copy-done((bf16[4096,128]{1,0:T(8,128)(2,1)S(1)}, bf16[4096,128]{1,0:T(8,128)(2,1)}, u32[]{:S(2)}) %copy-start) | copy-done | bytes 1048600
  2.5 0.0 copy-start.1
  2.6 1.2 %copy-done.1 = bf16[4096,128]{1,0:T(8,128)(2,1)S(1)} copy-done((bf16[4096,128]{1,0:T(8,128)(2,1)S(1)}, bf16[4096,128]{1,0:T(8,128)(2,1)}, u32[]{:S(2)}) %copy-start.1) | copy-done | bytes 1048600
  3.8 0.0 copy-start.2
  3.8 1.2 %copy-done.2 = bf16[128,4096]{1,0:T(8,128)(2,1)S(1)} copy-done((bf16[128,4096]{1,0:T(8,128)(2,1)S(1)}, bf16[128,4096]{1,0:T(8,128)(2,1)}, u32[]{:S(2)}) %copy-start.2) | copy-done | bytes 1048600
  5.0 0.0 copy-start.3
  5.0 0.9 copy-done.3
  6.0 0.0 copy-start.4
  6.0 0.7 copy-done.4
  6.7 0.0 copy-start.5
  6.7 0.7 copy-done.5
  7.4 93.9 %shard_map.91 = bf16[32,128]{1,0:T(8,128)(2,1)S(1)} custom-call(bf16[32,128]{1,0:T(8,128)(2,1)S(1)} %copy-done.5, bf16[512,256]{1,0:T(8,128)(2,1)S(1)} %copy-done.3, f32[1,4096]{1,0:T(1,128)S(1)} %bitcast.3, bf16[4096,128]{1,0:T(8,128)(2,1)S(1)} %copy-done, bf16[4096,128]{1,0:T(8,128)(2,1)S(1)} %copy-done.1, f32[1,128]{1,0:T(1,128)S(1)} %bitcast.4, ...), custom_call_target="tpu_custom_call" | custom-call | tf_op jit(solution)/shard_map/pallas_call | solution.py:476
  101.3 0.6 copy.12
Async XLA Ops:
  0.7 0.7 copy-start.6
  0.7 0.7 copy-start.7
  1.3 1.2 %copy-start = (bf16[4096,128]{1,0:T(8,128)(2,1)S(1)}, bf16[4096,128]{1,0:T(8,128)(2,1)}, u32[]{:S(2)}) copy-start(bf16[4096,128]{1,0:T(8,128)(2,1)} %wq_hbm.1) | copy-start | bytes 3145732
  2.5 1.2 %copy-start.1 = (bf16[4096,128]{1,0:T(8,128)(2,1)S(1)}, bf16[4096,128]{1,0:T(8,128)(2,1)}, u32[]{:S(2)}) copy-start(bf16[4096,128]{1,0:T(8,128)(2,1)} %wkv_hbm.1) | copy-start | bytes 3145732
  3.8 1.2 %copy-start.2 = (bf16[128,4096]{1,0:T(8,128)(2,1)S(1)}, bf16[128,4096]{1,0:T(8,128)(2,1)}, u32[]{:S(2)}) copy-start(bf16[128,4096]{1,0:T(8,128)(2,1)} %wo_hbm.1) | copy-start | bytes 3145732
  5.0 0.9 copy-start.3
  6.0 0.7 copy-start.4
  6.7 0.7 copy-start.5

commit v2 on v1

--- a/solution.py
+++ b/solution.py
@@ -34,13 +34,14 @@
 
 
 def kernel(
-    text_ref, vis_ref, gain_ref, wq_hbm, wkv_hbm, qg_ref, kg_ref, wo_hbm, gate_ref,
+    text_hbm, vis_ref, gain_hbm, wq_hbm, wkv_hbm, qg_hbm, kg_hbm, wo_hbm, gate_hbm,
     out_ref,
-    text_s, text_all, wq, wk, vb, q_loc, qbuf, kvst, kvb,
+    text_ref, gain_ref, qg_ref, kg_ref, gate_ref,
+    text_s, text_all, wq, wk, vb, q_loc, q_heads, qbuf, kvst, kvb,
     o_send, t_send, o_own, t_own, o_recv, t_recv, o2, t2, d_all, t_all,
     att, att_all, wo2, r_send, r_recv,
-    loc, vsend, vrecv, wsend, wrecv, tsend, trecv, txsend, txrecv, c1send, c1recv,
-    qsend, qfsend, qrecv, wosend, worecv, kvsend, kvrecv, osend, orecv, ssend, srecv,
+    loc, vsend, vrecv, wsend, wrecv, tsend, trecv, txsend, txrecv,
+    qzsend, qzrecv, qsend, qrecv, wosend, worecv, kvsend, kvrecv, osend, orecv, ssend, srecv,
     dsend, drecv, t2send, t2recv, asend, arecv, rsend, rrecv,
 ):
     t = lax.axis_index("text")
@@ -61,11 +62,12 @@
     far = (t + 8) % 16
     col = t - c
     far_sib = (sib + 8) % 16
+    cross = jnp.where((t // 4) % 2 == 0, dn, up)
+    group = half * 8
     t1 = half * 8 + v // 4
     v1 = g * 4 + v % 4
     v2 = g * 4 + (v % 4) + 1 - 2 * (v % 2)
     owner = g == v // 4
-    j_own = v % 4
 
     def at_z(zz):
         return 2 * zz + xl
@@ -83,39 +85,48 @@
     own_tokens = pltpu.make_async_copy(vis_ref.at[pl.ds(c * 256, 256), :], vb.at[t], loc.at[0])
     own_wq = pltpu.make_async_copy(wq_hbm, wq, loc.at[1])
     own_wk = pltpu.make_async_copy(wkv_hbm, wk.at[:, pl.ds(pl.multiple_of(c * 128, 128), 128)], loc.at[2])
+    small = [
+        pltpu.make_async_copy(text_hbm, text_ref, loc.at[4]),
+        pltpu.make_async_copy(
+            gain_hbm.at[:, pl.ds(pl.multiple_of(v * 128, 128), 128)], gain_ref, loc.at[5]
+        ),
+        pltpu.make_async_copy(qg_hbm, qg_ref, loc.at[6]),
+        pltpu.make_async_copy(kg_hbm, kg_ref, loc.at[7]),
+        pltpu.make_async_copy(gate_hbm, gate_ref, loc.at[8]),
+    ]
+    for copy in small:
+        copy.start()
     own_tokens.start()
     own_wk.start()
     own_wq.start()
-    gain = gain_ref[:, pl.ds(pl.multiple_of(v * 128, 128), 128)]
-    text_s[...] = (text_ref[...].astype(F32) * gain).astype(BF16)
+    barrier = pltpu.get_barrier_semaphore()
+
+    def greet(tt, vv):
+        pl.semaphore_signal(barrier, inc=1, device_id=(tt, vv), device_id_type=MESH)
+
+    def greet_group(i, carry):
+        other = group + lax.rem(g + i, 8)
+        greet(other, v)
+        greet(other, vx)
+        return carry
+
+    for other in (far, far_sib, cross):
+        greet(other, v)
+    greet(t, vx)
+    lax.fori_loop(1, 8, greet_group, 0)
+    each_z(lambda zz: greet(t, at_z(zz)))
+
+    @pl.when(jnp.logical_not(owner))
+    def _():
+        greet(t1, v1)
+        greet(t1, v2)
+
+    for copy in small:
+        copy.wait()
+    text_s[...] = (text_ref[...].astype(F32) * gain_ref[...]).astype(BF16)
     my_cols = pl.ds(pl.multiple_of(z * 128, 128), 128)
     text_all[xl, :, my_cols] = text_s[...]
-
-    barrier = pltpu.get_barrier_semaphore()
-
-    def greet(tt, vv):
-        pl.semaphore_signal(barrier, inc=1, device_id=(tt, vv), device_id_type=MESH)
-
-    each_z(lambda zz: greet(t, at_z(zz)))
-    greet(t, vx)
-    for other in (sib, xp, up, dn, far, far_sib):
-        greet(other, v)
-    greet(t1, v2)
-
-    @pl.when(owner)
-    def _():
-        def step(i, carry):
-            greet(half * 8 + lax.rem(g + i, 8), v)
-            return carry
-
-        lax.fori_loop(1, 8, step, 0)
-
-    @pl.when(jnp.logical_not(owner))
-    def _():
-        greet(t1, v)
-        greet(t1, v1)
-
-    pl.semaphore_wait(barrier, 15 + 1 + 6 + 1 + jnp.where(owner, 7, 2))
+    pl.semaphore_wait(barrier, 3 + 1 + 14 + 15 + jnp.where(owner, 0, 2))
 
     rows_here = pl.ds(c * 256, 256)
     rows_sib = pl.ds((1 - c) * 256, 256)
@@ -155,27 +166,28 @@
     for target in (up, dn, xp):
         send_block(sib, target)
 
-    z_bytes = text_all.at[0, :, pl.ds(0, 15 * 128)]
-    rcopy(z_bytes, z_bytes, tsend, trecv, t, vx).wait_recv()
-    text_x = rcopy(text_all.at[xl], text_all.at[xl], txsend, txrecv, t, vx)
-    text_x.start()
-
-    got(xp)
-    for target in (up, dn):
-        send_block(xp, target)
-    got(xps)
-    for target in (up, dn):
-        send_block(xps, target)
-
     up0, up1 = (col + 4) % 16, (col + 5) % 16
     dn0, dn1 = (col + 12) % 16, (col + 13) % 16
     pcol = base + (1 - xh) * 2
     pup0, pup1 = (pcol + 4) % 16, (pcol + 5) % 16
     pdn0, pdn1 = (pcol + 12) % 16, (pcol + 13) % 16
-    got(dn0)
-    send_block(dn0, up)
-    got(up1)
-    send_block(up1, dn)
+
+    def relay(f, target):
+        got(f)
+        send_block(f, target)
+
+    relay(dn0, up)
+    relay(up1, dn)
+    relay(pcol, up)
+    relay(pcol + 1, dn)
+
+    z_bytes = text_all.at[0, :, pl.ds(0, 15 * 128)]
+    rcopy(z_bytes, z_bytes, tsend, trecv, t, vx).wait_recv()
+    text_x = rcopy(text_all.at[xl], text_all.at[xl], txsend, txrecv, t, vx)
+    text_x.start()
+
+    relay(dn1, xp)
+    relay(up0, xp)
 
     text_other = text_all.at[1 - xl]
     rcopy(text_other, text_other, txsend, txrecv, t, vx).wait_recv()
@@ -187,17 +199,15 @@
         )
         q = q + jnp.dot(lhs, wq[k * 256 : k * 256 + 256, :], preferred_element_type=F32)
     q_loc[...] = head_norm(q, qg_ref[...]).astype(BF16)
-    my_rows = pl.ds(pl.multiple_of(g * 32, 32), 32)
-    c1 = rcopy(q_loc, qbuf.at[j_own, my_rows, :], c1send, c1recv.at[g], t1, v)
-
-    @pl.when(jnp.logical_not(owner))
-    def _():
-        c1.start()
-
-    got(pdn0)
-    send_block(pdn0, up)
-    got(pup1)
-    send_block(pup1, dn)
+    q_heads[z] = q_loc[...]
+
+    def push_q(zz):
+        rcopy(q_loc, q_heads.at[z], qzsend, qzrecv, t, at_z(zz)).start()
+
+    each_z(push_q)
+
+    relay(pdn0, up)
+    relay(pup1, dn)
 
     def wo_step(zz, carry):
         src_own = wo_hbm.at[:, pl.ds(pl.multiple_of((2 * zz + xl) * 128, 128), 128)]
@@ -207,24 +217,6 @@
         rcopy(src_out, dst, wosend, worecv, t, vx).start()
         return carry
 
-    q_own = qbuf.at[j_own]
-
-    def push_q(zz):
-        rcopy(q_own, q_own, qsend, qrecv.at[j_own], t, at_z(zz)).start()
-
-    @pl.when(owner)
-    def _():
-        qbuf[j_own, my_rows, :] = q_loc[...]
-
-        def step(i, carry):
-            s = lax.rem(g + i, 8)
-            part = qbuf.at[j_own, pl.ds(pl.multiple_of(s * 32, 32), 32), :]
-            rcopy(part, part, c1send, c1recv.at[s], t1, v).wait_recv()
-            return carry
-
-        lax.fori_loop(1, 8, step, 0)
-        each_z(push_q)
-
     lax.fori_loop(0, 16, wo_step, 0)
 
     own_tokens.wait()
@@ -233,28 +225,26 @@
     rcopy(wk_other, wk_other, wsend, wrecv, sib, v).wait_recv()
     acc = add(acc, t)
     acc = add(acc, sib)
-    acc = add(acc, xp)
-    acc = add(acc, xps)
-    acc = add(acc, dn0)
-    acc = add(acc, up1)
-    acc = add(acc, pdn0)
-    acc = add(acc, pup1)
-    for f in (dn1, up0, pdn1, pup0):
-        got(f)
+    for f in (pcol, pcol + 1, dn0, up1, dn1, up0, pdn0, pup1):
         acc = add(acc, f)
 
-    for jj in range(2):
-        j = 2 * jj + xl
-
-        @pl.when(v != 4 * g + j)
-        def _():
-            rcopy(qbuf.at[j], qbuf.at[j], qsend, qrecv.at[j], t, vx).wait_recv()
-
-        rcopy(qbuf.at[j], qbuf.at[j], qfsend.at[jj], qrecv.at[j], t, vx).start()
+    q15 = q_heads.at[pl.ds(0, 15)]
+    rcopy(q15, q15, qzsend, qzrecv, t, vx).wait_recv()
+
+    def share_heads(i, carry):
+        other = lax.rem(g + i, 8)
+        part = q_heads.at[pl.ds(2 * other, 2)]
+        rcopy(part, qbuf.at[xl, g], qsend, qrecv.at[xl], group + other, v).start()
+        rcopy(part, qbuf.at[xl, g], qsend, qrecv.at[xl], group + other, vx).start()
+        return carry
+
+    lax.fori_loop(1, 8, share_heads, 0)
+    rcopy(q_heads.at[pl.ds(2 * g, 2)], qbuf.at[xl, g], qsend, qrecv.at[xl], t, vx).start()
+    qbuf[xl, g] = q_heads[pl.ds(2 * g, 2)]
 
     far0, far1 = (col + 8) % 16, (col + 9) % 16
     pfar0, pfar1 = (pcol + 8) % 16, (pcol + 9) % 16
-    for f in (far0, far1, pfar0, pfar1):
+    for f in (pdn1, pup0, far0, far1, pfar0, pfar1):
         got(f)
         acc = add(acc, f)
 
@@ -274,16 +264,18 @@
     kv_sib.start()
     kvb[half, my_half, :] = kvst[c]
 
-    for jj in range(2):
-        j = 2 * jj + 1 - xl
-        rcopy(qbuf.at[j], qbuf.at[j], qsend, qrecv.at[j], t, vx).wait_recv()
+    q7 = qbuf.at[xl, pl.ds(0, 7)]
+    rcopy(q7, q7, qsend, qrecv.at[xl], t, vx).wait_recv()
+    q8 = qbuf.at[1 - xl]
+    rcopy(q8, q8, qsend, qrecv.at[1 - xl], t, vx).wait_recv()
     rcopy(kvst.at[0], kvb.at[half, other_half, :], kvsend.at[0], kvrecv.at[0], sib, v).wait_recv()
     rcopy(kvst.at[0], kvb.at[1 - half, my_half, :], kvsend.at[1], kvrecv.at[1], far, v).wait_recv()
     rcopy(kvst.at[0], kvb.at[1 - half, other_half, :], kvsend.at[2], kvrecv.at[2], far, v).wait_recv()
 
-    def attend(j):
+    def attend(parity, jj):
+        queries = qbuf[parity, :, jj].reshape(256, 128)
         scores = lax.dot_general(
-            qbuf[j], kvb[0], (((1,), (1,)), ((), ())), preferred_element_type=F32
+            queries, kvb[0], (((1,), (1,)), ((), ())), preferred_element_type=F32
         )
         peak = jnp.max(scores, axis=-1, keepdims=True)
         probs = jnp.exp2((scores - peak) * SCALE_LOG2)
@@ -293,7 +285,7 @@
 
     o_out = []
     for jj in range(2):
-        partial, tile = attend(2 * jj + 1 - xl)
+        partial, tile = attend(1 - xl, jj)
         o_send[jj] = partial.astype(BF16)
         t_send[jj] = tile
         copy = rcopy(o_send.at[jj], o_recv.at[jj], osend.at[jj], orecv.at[jj], t, vx)
@@ -303,7 +295,7 @@
         copy.start()
         o_out.append(copy)
     for jj in range(2):
-        partial, tile = attend(2 * jj + xl)
+        partial, tile = attend(xl, jj)
         o_own[jj] = partial
         t_own[jj] = tile
 
@@ -391,7 +383,7 @@
     summed = r_recv[0].astype(F32)
     for s in range(1, 16):
         summed = summed + r_recv[s].astype(F32)
-    out_ref[...] = (jnp.tanh(jnp.full((32, 128), gate_ref[0], F32)) * summed).astype(BF16)
+    out_ref[...] = (jnp.tanh(gate_ref[...]) * summed).astype(BF16)
 
     for copy in sends:
         copy.wait_send()
@@ -401,19 +393,11 @@
 
     @pl.when(jnp.logical_not(owner))
     def _():
-        c1.wait_send()
         a1.wait_send()
 
-    @pl.when(owner)
-    def _():
-        def step(i, carry):
-            rcopy(q_own, q_own, qsend, qrecv.at[j_own], t, vx).wait_send()
-            return carry
-
-        lax.fori_loop(0, 15, step, 0)
-
-    for jj in range(2):
-        rcopy(qbuf.at[0], qbuf.at[0], qfsend.at[jj], qrecv.at[0], t, vx).wait_send()
+    rcopy(q15, q15, qzsend, qzrecv, t, vx).wait_send()
+    rcopy(q7, q7, qsend, qrecv.at[xl], t, vx).wait_send()
+    rcopy(q8, q8, qsend, qrecv.at[xl], t, vx).wait_send()
     rcopy(wo2.at[xl], wo2.at[xl], wosend, worecv, t, vx).wait_send()
     for copy in (kv_sib, kv_far, kv_far_sib, a2, *o_out):
         copy.wait_send()
@@ -427,19 +411,24 @@
 ):
     vmem = pl.BlockSpec(memory_space=pltpu.VMEM)
     hbm = pl.BlockSpec(memory_space=pl.ANY)
-    smem = pl.BlockSpec(memory_space=pltpu.SMEM)
     dma = pltpu.SemaphoreType.DMA
     one = dma(())
     buffers = [
-        pltpu.VMEM(shape, dtype)
-        for shape, dtype in (
+        pltpu.VMEM(*buffer)
+        for buffer in (
+            ((32, 128), BF16),
+            ((1, 128), F32),
+            ((1, 128), F32),
+            ((1, 128), F32),
+            ((1, 1), F32),
             ((32, 128), BF16),
             ((2, 32, 2048), BF16),
             ((4096, 128), BF16),
             ((4096, 256), BF16),
             ((16, 256, 256), BF16),
             ((32, 128), BF16),
-            ((4, 256, 128), BF16),
+            ((16, 32, 128), BF16),
+            ((2, 8, 2, 32, 128), BF16),
             ((2, 256, 128), BF16),
             ((2, 512, 128), BF16),
             ((2, 256, 128), BF16),
@@ -460,12 +449,11 @@
         )
     ]
     semaphores = [
-        dma((4,)),
+        dma((9,)),
         dma((15,)), dma((16,)),
         one, one,
         one, one, one, one,
-        one, dma((8,)),
-        one, dma((2,)), dma((4,)),
+        one, one, one, dma((2,)),
         one, one,
         dma((3,)), dma((3,)),
         dma((2,)), dma((2,)), dma((2,)), dma((2,)),
@@ -476,15 +464,15 @@
     return pl.pallas_call(
         kernel,
         out_shape=jax.ShapeDtypeStruct((32, 128), BF16),
-        in_specs=[vmem, hbm, vmem, hbm, hbm, vmem, vmem, hbm, smem],
+        in_specs=[hbm] * 9,
         out_specs=vmem,
         scratch_shapes=buffers + semaphores,
         compiler_params=pltpu.CompilerParams(
-            collective_id=0, has_side_effects=True, vmem_limit_bytes=48 * 1024 * 1024
+            collective_id=0, has_side_effects=True, vmem_limit_bytes=60 * 1024 * 1024
         ),
     )(
         text_rows, visual, norm_gain.reshape(1, -1), q_weight, key_value_weight,
-        q_gain.reshape(1, -1), k_gain.reshape(1, -1), out_weight, attn_gate,
+        q_gain.reshape(1, -1), k_gain.reshape(1, -1), out_weight, attn_gate.reshape(1, 1),
     )
 
 

time: 102 us -> 86.8 us (0.85)
  the two profiles are of different devices: /device:TPU:8 before, /device:TPU:16 now
where the time goes in v2:
time: 86.8 us; the launch traced here: 86.5 us
  Pallas kernels  84.6 us (97%)
  local copies, waits for them, and re-layouts  1.3 us (1%)
    pallas_call x1, Pallas kernels, on_device(): pl.pallas_call(kernel, out_shape=jax.ShapeDtypeStruct((32, 128), BF16), i...  84.6 us

profile of v2, /device:TPU:16, one launch (start us, length us, event | category | flops | bytes accessed | tf_op | source)
XLA Modules:
  0.0 86.5 jit_solution(4820111519494582507)
XLA Ops:
  0.7 84.6 %shard_map.91 = bf16[32,128]{1,0:T(8,128)(2,1)} custom-call(bf16[32,128]{1,0:T(8,128)(2,1)} %text_hbm.1, bf16[512,256]{1,0:T(8,128)(2,1)} %vis_ref.1, f32[1,4096]{1,0:T(1,128)} %bitcast.5, bf16[4096,128]{1,0:T(8,128)(2,1)} %wq_hbm.1, bf16[4096,128]{1,0:T(8,128)(2,1)} %wkv_hbm.1, f32[1,128]{1,0:T(1,128)} %bitcast.6, f32[1,128]{1,0:T(1,128)} %bitcast.7, ...), custom_call_target="tpu_custom_call" | custom-call | tf_op jit(solution)/shard_map/pallas_call | solution.py:464
  85.2 1.3 %copy.12 = bf16[32,128]{1,0:T(8,128)(2,1)} copy(bf16[32,128]{1,0:T(8,128)(2,1)} %shard_map.91) | data formatting | bytes 16384

commit v3 on v2

v3 whole, which is shorter than its diff:
```python
import jax
import jax.numpy as jnp
from jax import lax
from jax.experimental import pallas as pl
from jax.experimental.pallas import tpu as pltpu
from jax.sharding import PartitionSpec as P

HEAD = 128
EPS = 1e-05
SCALE_LOG2 = (HEAD ** -0.5) * 1.4426950408889634
MESH = pl.DeviceIdType.MESH
BF16 = jnp.bfloat16
F32 = jnp.float32


def rcopy(src, dst, send, recv, t, v):
    return pltpu.make_async_remote_copy(
        src_ref=src, dst_ref=dst, send_sem=send, recv_sem=recv, device_id=(t, v), device_id_type=MESH
    )


def head_norm(heads, gain):
    mean_square = jnp.mean(heads * heads, axis=-1, keepdims=True)
    return heads * lax.rsqrt(mean_square + EPS) * gain


def column_tile(columns):
    lane = lax.broadcasted_iota(jnp.int32, (8, 128), 1)
    tile = jnp.zeros((8, 128), F32)
    for i, column in enumerate(columns):
        for k in range(32):
            tile = jnp.where(lane == 32 * i + k, column[8 * k : 8 * k + 8], tile)
    return tile


def kernel(
    text_hbm, vis_ref, gain_hbm, wq_hbm, wkv_hbm, qg_hbm, kg_hbm, wo_hbm, gate_hbm,
    out_ref,
    text_ref, gain_ref, qg_ref, kg_ref, gate_ref,
    text_s, text_all, wq, wk, vb, q_loc, q_heads, qbuf, kvst, kvb,
    o_send, t_send, o_recv, t_recv, o2, t2, d_all, t_all, att, att_all, wo_all,
    loc, vsend, vrecv, wsend, wrecv, tsend, trecv, txsend, txrecv,
    qzsend, qzrecv, qsend, qrecv, kvsend, kvrecv, osend, orecv, ssend, srecv,
    dsend, drecv, t2send, t2recv, asend, arecv, axsend, axrecv,
    wzsend, wzrecv, wpsend, wprecv, wssend, wsrecv,
):
    t = lax.axis_index("text")
    v = lax.axis_index("vis")
    z = v // 2
    xl = v % 2
    c = t % 2
    half = t // 8
    g = t % 8
    vx = 2 * z + 1 - xl
    sib = t + 1 - 2 * c
    xh = (t // 2) % 2
    base = (t // 4) * 4
    xp = base + (1 - xh) * 2 + c
    up = (t + 4) % 16
    dn = (t + 12) % 16
    far = (t + 8) % 16
    col = t - c
    pcol = base + (1 - xh) * 2
    far_sib = (sib + 8) % 16
    cross = jnp.where((t // 4) % 2 == 0, dn, up)
    group = half * 8
    own_half = half == 0

    def at_z(zz):
        return 2 * zz + xl

    def each_z(body):
        def step(i, carry):
            body(lax.rem(z + 8 + jnp.where(i % 2 == 0, -(i // 2), (i + 1) // 2), 16), i)
            return carry

        lax.fori_loop(0, 15, step, 0)

    def lanes(i):
        return pl.ds(pl.multiple_of(i * 128, 128), 128)

    small = [
        pltpu.make_async_copy(text_hbm, text_ref, loc.at[4]),
        pltpu.make_async_copy(gain_hbm.at[:, lanes(v)], gain_ref, loc.at[5]),
        pltpu.make_async_copy(qg_hbm, qg_ref, loc.at[6]),
        pltpu.make_async_copy(kg_hbm, kg_ref, loc.at[7]),
        pltpu.make_async_copy(gate_hbm, gate_ref, loc.at[8]),
    ]
    for copy in small:
        copy.start()
    own_tokens = pltpu.make_async_copy(vis_ref.at[pl.ds(c * 256, 256), :], vb.at[t], loc.at[0])
    own_wq = pltpu.make_async_copy(wq_hbm, wq, loc.at[1])
    own_wk = pltpu.make_async_copy(wkv_hbm, wk.at[:, lanes(c)], loc.at[2])
    own_tokens.start()
    own_wk.start()
    own_wq.start()

    barrier = pltpu.get_barrier_semaphore()

    def greet(tt, vv):
        pl.semaphore_signal(barrier, inc=1, device_id=(tt, vv), device_id_type=MESH)

    def greet_group(i, carry):
        other = group + lax.rem(g + i, 8)
        greet(other, v)
        greet(other, vx)
        return carry

    for other in (far, far_sib, cross):
        greet(other, v)
    greet(t, vx)
    lax.fori_loop(1, 8, greet_group, 0)
    each_z(lambda zz, i: greet(t, at_z(zz)))

    @pl.when(c == 1)
    def _():
        each_z(lambda zz, i: greet(t, 2 * zz + 1 - xl))

    for copy in small:
        copy.wait()
    text_s[...] = (text_ref[...].astype(F32) * gain_ref[...]).astype(BF16)
    text_all[xl, :, lanes(z)] = text_s[...]
    pl.semaphore_wait(barrier, 3 + 1 + 14 + 15 + 15 * c)

    def push_columns(block, everything, send, recv):
        def push(zz, i):
            near = jnp.where(i < 7, 1, 0)
            rcopy(block, everything.at[xl, :, lanes(z)], send, recv.at[near], t, at_z(zz)).start()

        each_z(push)

    def forward_columns(everything, recv, xsend, xrecv, far_group):
        count = 7 if far_group else 8
        part = everything.at[0, :, pl.ds(0, count * 128)]
        rcopy(part, part, xsend, recv.at[far_group], t, vx).wait_recv()

        def forward(i, carry):
            mine = everything.at[xl, :, lanes(lax.rem(z + i, 16))]
            rcopy(mine, mine, xsend, xrecv, t, vx).start()
            return carry

        lax.fori_loop(*((5, 12) if far_group else (12, 21)), forward, 0)

    push_columns(text_s, text_all, tsend, trecv)

    sends = []

    def piece(f, h):
        return vb.at[f, pl.ds(h * 128, 128), :]

    def send_block(f, h, target, src=None):
        copy = rcopy(
            piece(f, h) if src is None else src, piece(f, h),
            vsend.at[len(sends)], vrecv.at[f + 16 * h], target, v,
        )
        copy.start()
        sends.append(copy)

    def got(f, h):
        rcopy(piece(f, h), piece(f, h), vsend.at[0], vrecv.at[f + 16 * h], sib, v).wait_recv()

    def relay(f, h, *targets):
        got(f, h)
        for target in targets:
            send_block(f, h, target)

    for h in range(2):
        send_block(t, h, sib, vis_ref.at[pl.ds((1 - c) * 256 + h * 128, 128), :])
        for target in (up, dn, xp):
            send_block(t, h, target, vis_ref.at[pl.ds(c * 256 + h * 128, 128), :])
    w_out = rcopy(wkv_hbm, wk.at[:, lanes(c)], wsend, wrecv, sib, v)
    w_out.start()
    for h in range(2):
        relay(sib, h, up, dn, xp)

    up0, up1 = (col + 4) % 16, (col + 5) % 16
    dn0, dn1 = (col + 12) % 16, (col + 13) % 16
    far0, far1 = (col + 8) % 16, (col + 9) % 16
    pup0, pup1 = (pcol + 4) % 16, (pcol + 5) % 16
    pdn0, pdn1 = (pcol + 12) % 16, (pcol + 13) % 16
    pfar0, pfar1 = (pcol + 8) % 16, (pcol + 9) % 16

    def relays_first(h):
        relay(dn0, h, up)
        relay(up1, h, dn)
        relay(pcol, h, up)
        relay(pcol + 1, h, dn)

    def relays_second(h):
        relay(dn1, h, xp)
        relay(up0, h, xp)
        relay(pdn0, h, up)
        relay(pup1, h, dn)

    forward_columns(text_all, trecv, txsend, txrecv, 0)
    relays_first(0)
    forward_columns(text_all, trecv, txsend, txrecv, 1)
    relays_second(0)

    text_other = text_all.at[1 - xl]
    rcopy(text_other, text_other, txsend, txrecv, t, vx).wait_recv()
    own_wq.wait()
    q = jnp.zeros((32, 128), F32)
    for k in range(16):
        lhs = jnp.concatenate(
            [text_all[0, :, k * 128 : k * 128 + 128], text_all[1, :, k * 128 : k * 128 + 128]], axis=1
        )
        q = q + jnp.dot(lhs, wq[k * 256 : k * 256 + 256, :], preferred_element_type=F32)
    q_loc[...] = head_norm(q, qg_ref[...]).astype(BF16)
    q_heads[z] = q_loc[...]
    each_z(
        lambda zz, i: rcopy(
            q_loc, q_heads.at[z], qzsend, qzrecv.at[z], t, at_z(zz)
        ).start()
    )

    w_rows = pl.ds(pl.multiple_of((t // 2) * 16, 16), 16)
    qw = (xl + c) % 2

    def push_w(zz):
        rcopy(
            wo_hbm.at[w_rows, lanes(2 * zz + qw)], wo_all.at[xl, z, w_rows, :],
            wzsend, wzrecv, t, 2 * zz + qw,
        ).start()

    own_w = pltpu.make_async_copy(
        wo_hbm.at[w_rows, lanes(v)], wo_all.at[xl, z, w_rows, :], loc.at[3]
    )
    each_z(lambda zz, i: push_w(zz))

    @pl.when(c == 0)
    def _():
        own_w.start()

    @pl.when(c == 1)
    def _():
        push_w(z)

    relays_first(1)
    relays_second(1)

    def share_heads(i, carry):
        other = lax.rem(z // 2 + 8 + jnp.where(i % 2 == 0, -(i // 2), (i + 1) // 2), 8)
        for e in range(2):
            zz = 2 * other + e

            @pl.when(zz != z)
            def _():
                rcopy(q_loc, q_heads.at[zz], qzsend, qzrecv.at[zz], t, vx).wait_recv()

        part = q_heads.at[pl.ds(2 * other, 2)]
        rcopy(part, qbuf.at[xl, g], qsend, qrecv.at[xl], group + other, vx).start()

        @pl.when(other != g)
        def _():
            rcopy(part, qbuf.at[xl, g], qsend, qrecv.at[xl], group + other, v).start()

        @pl.when(other == g)
        def _():
            qbuf[xl, g] = q_heads[pl.ds(2 * g, 2)]

        return carry

    lax.fori_loop(0, 4, share_heads, 0)

    own_tokens.wait()
    own_wk.wait()
    wk_other = wk.at[:, lanes(1 - c)]
    rcopy(wk_other, wk_other, wsend, wrecv, sib, v).wait_recv()
    kv_sends = []

    def project(h):
        for f in (pdn1, pup0, far0, far1, pfar0, pfar1):
            got(f, h)
        acc = jnp.zeros((128, 256), F32)
        for f in range(16):
            acc = acc + jnp.dot(
                vb[f, h * 128 : h * 128 + 128, :], wk[f * 256 : f * 256 + 256, :],
                preferred_element_type=F32,
            )
        raw = acc.astype(BF16).astype(F32)
        for n in range(2):
            part = raw[:, n * 128 : n * 128 + 128]
            normed = head_norm(part, kg_ref[...])
            kvst[h, n] = jnp.where(own_half, normed, part).astype(BF16)
        rows = pl.ds(pl.multiple_of(c * 256 + h * 128, 128), 128)
        for i, (n, target) in enumerate(((c, far), (1 - c, far_sib), (1 - c, sib))):
            copy = rcopy(
                kvst.at[h, n], kvb.at[half, rows, :], kvsend.at[3 * h + i], kvrecv.at[3 * h + i], target, v
            )
            copy.start()
            kv_sends.append(copy)
        kvb[half, rows, :] = kvst[h, c]

    project(0)
    lax.fori_loop(4, 8, share_heads, 0)
    project(1)

    def w_block(f):
        return wo_all.at[qw, :, pl.ds(pl.multiple_of((f // 2) * 16, 16), 16), :]

    w_sends = []

    def w_send(f, *targets):
        for target in targets:
            copy = rcopy(w_block(f), w_block(f), wpsend.at[len(w_sends)], wprecv.at[f // 2], target, v)
            copy.start()
            w_sends.append(copy)

    def w_got(f):
        rcopy(w_block(f), w_block(f), wpsend.at[0], wprecv.at[f // 2], sib, v).wait_recv()

    def w_landed(count):
        return wo_all.at[qw, pl.ds(0, count), pl.ds(0, 16), :]

    @pl.when(c == 0)
    def _():
        own_w.wait()
        rcopy(w_landed(15), w_landed(15), wzsend, wzrecv, t, vx).wait_recv()

    @pl.when(c == 1)
    def _():
        rcopy(w_landed(16), w_landed(16), wzsend, wzrecv, t, vx).wait_recv()

    w_send(t, xp, up, dn)

    q7 = qbuf.at[xl, pl.ds(0, 7)]
    rcopy(q7, q7, qsend, qrecv.at[xl], t, vx).wait_recv()
    q8 = qbuf.at[1 - xl]
    rcopy(q8, q8, qsend, qrecv.at[1 - xl], t, vx).wait_recv()
    for h in range(2):
        here = pl.ds(pl.multiple_of(c * 256 + h * 128, 128), 128)
        there = pl.ds(pl.multiple_of((1 - c) * 256 + h * 128, 128), 128)
        for i, rows in ((0, (1 - half, here)), (1, (1 - half, there)), (2, (half, there))):
            block = kvb.at[rows[0], rows[1], :]
            rcopy(block, block, kvsend.at[0], kvrecv.at[3 * h + i], sib, v).wait_recv()

    def attend(parity):
        columns = []
        for jj in range(2):
            scores = lax.dot_general(
                qbuf[parity, :, jj].reshape(256, 128), kvb[0], (((1,), (1,)), ((), ())),
                preferred_element_type=F32,
            )
            peak = jnp.max(scores, axis=-1, keepdims=True)
            probs = jnp.exp2((scores - peak) * SCALE_LOG2)
            columns += [peak * SCALE_LOG2, jnp.sum(probs, axis=-1, keepdims=True)]
            partial = jnp.dot(probs.astype(BF16), kvb[1], preferred_element_type=F32)
            o_send[parity, :, jj] = partial.astype(BF16).reshape(8, 32, 128)
        t_send[parity] = column_tile(columns)

    def send_partial(parity, rb, vv):
        rcopy(
            o_send.at[parity, rb], o_recv.at[xl, g], osend, orecv.at[xl, g], group + rb, vv
        ).start()
        rcopy(
            t_send.at[parity], t_recv.at[xl, g], ssend, srecv.at[xl, g], group + rb, vv
        ).start()

    def send_other(i, carry):
        send_partial(1 - xl, lax.rem(g + i, 8), vx)
        return carry

    def send_own(i, carry):
        send_partial(xl, lax.rem(g + i, 8), v)
        return carry

    attend(1 - xl)
    lax.fori_loop(0, 8, send_other, 0)
    attend(xl)
    lax.fori_loop(1, 8, send_own, 0)
    o_recv[xl, g] = o_send[xl, g]
    t_recv[xl, g] = t_send[xl]

    w_got(xp)
    w_send(xp, up, dn)
    w_got(dn)
    w_send(dn, up)

    lane = lax.broadcasted_iota(jnp.int32, (8, 128), 1)
    sub = lax.broadcasted_iota(jnp.int32, (8, 128), 0)

    def merge(i, carry):
        src = lax.rem(g + i, 8)
        for x in range(2):

            @pl.when(jnp.logical_or(x != xl, src != g))
            def _():
                rcopy(o_recv.at[x, src], o_recv.at[x, src], osend, orecv.at[x, src], t, vx).wait_recv()
                rcopy(t_recv.at[x, src], t_recv.at[x, src], ssend, srecv.at[x, src], t, vx).wait_recv()

        shift = lax.rem(128 - 4 * g, 128)
        first = pltpu.roll(t_recv[0, src], shift, 1)
        second = pltpu.roll(t_recv[1, src], shift, 1)
        top = jnp.maximum(first, second)
        a = jnp.exp2(first - top)
        b = jnp.exp2(second - top)
        total = pltpu.roll(a, 32, 1) * first + pltpu.roll(b, 32, 1) * second
        for jj in range(2):
            zz = 2 * src + jj
            row = jnp.zeros((8, 128), F32)
            blocks = []
            for k in range(4):
                m, l = 64 * jj + k, 64 * jj + 32 + k
                row = jnp.where(lane == 8 * sub + k, top[:, m : m + 1], row)
                row = jnp.where(lane == 8 * sub + 4 + k, total[:, l : l + 1], row)
                rows = slice(8 * k, 8 * k + 8)
                blocks.append(
                    o_recv[0, src, jj].astype(F32)[rows] * a[:, m : m + 1]
                    + o_recv[1, src, jj].astype(F32)[rows] * b[:, m : m + 1]
                )
            o2[zz] = jnp.concatenate(blocks, axis=0).astype(BF16)
            t2[zz, 0:1, :] = jnp.sum(row, axis=0, keepdims=True)

            @pl.when(zz != z)
            def _():
                rcopy(o2.at[zz], d_all.at[z], dsend, drecv, t, at_z(zz)).start()
                rcopy(
                    t2.at[zz, pl.ds(0, 1), :], t_all.at[z, pl.ds(0, 1), :], t2send, t2recv, t, at_z(zz)
                ).start()

            @pl.when(zz == z)
            def _():
                d_all[z] = o2[zz]
                t_all[z, 0:1, :] = t2[zz, 0:1, :]

        return carry

    lax.fori_loop(0, 8, merge, 0)

    w_got(far)
    w_send(far, xp)

    d15, t15 = d_all.at[pl.ds(0, 15)], t_all.at[pl.ds(0, 15), pl.ds(0, 1), :]
    rcopy(t15, t15, t2send, t2recv, t, vx).wait_recv()
    rcopy(d15, d15, dsend, drecv, t, vx).wait_recv()
    top = t_all[0, 0:1, :]
    for s in range(1, 16):
        top = jnp.maximum(top, t_all[s, 0:1, :])

    def column(row, k):
        return jnp.sum(
            jnp.where(lane == 8 * sub + k, jnp.broadcast_to(row, (8, 128)), 0.0), axis=1, keepdims=True
        )

    den = jnp.zeros((1, 128), F32)
    num = [jnp.zeros((8, 128), F32) for _ in range(4)]
    for s in range(16):
        row = t_all[s, 0:1, :]
        w = jnp.exp2(row - top)
        den = den + w * pltpu.roll(row, 124, 1)
        block = d_all[s].astype(F32)
        for k in range(4):
            num[k] = num[k] + block[8 * k : 8 * k + 8] * column(w, k)
    attended = jnp.concatenate([num[k] / column(den, k) for k in range(4)], axis=0)
    att[...] = attended.astype(BF16)
    att_all[xl, :, lanes(z)] = att[...]
    push_columns(att, att_all, asend, arecv)

    for f in (up, pup0, pdn0, pfar0):
        w_got(f)
    w_sib = rcopy(wo_all.at[qw], wo_all.at[qw], wssend, wsrecv, sib, v)
    w_sib.start()

    forward_columns(att_all, arecv, axsend, axrecv, 0)
    forward_columns(att_all, arecv, axsend, axrecv, 1)
    rcopy(wo_all.at[1 - qw], wo_all.at[1 - qw], wssend, wsrecv, sib, v).wait_recv()
    att_other = att_all.at[1 - xl]
    rcopy(att_other, att_other, axsend, axrecv, t, vx).wait_recv()
    summed = jnp.zeros((32, 128), F32)
    for n in range(2):
        for k in range(8):
            summed = summed + jnp.dot(
                att_all[n, :, k * 256 : k * 256 + 256],
                wo_all[n, 2 * k : 2 * k + 2].reshape(256, 128),
                preferred_element_type=F32,
            )
    out_ref[...] = (jnp.tanh(gate_ref[...]) * summed).astype(BF16)

    for copy in (*sends, w_out, *kv_sends, *w_sends, w_sib):
        copy.wait_send()
    for everything, send, xsend in ((text_all, tsend, txsend), (att_all, asend, axsend)):
        block = everything.at[0, :, pl.ds(0, 15 * 128)]
        rcopy(block, block, send, trecv.at[0], t, vx).wait_send()
        rcopy(everything.at[0], everything.at[0], xsend, trecv.at[0], t, vx).wait_send()
    q15 = q_heads.at[pl.ds(0, 15)]
    rcopy(q15, q15, qzsend, qzrecv.at[0], t, vx).wait_send()
    rcopy(q7, q7, qsend, qrecv.at[xl], t, vx).wait_send()
    rcopy(q8, q8, qsend, qrecv.at[xl], t, vx).wait_send()
    o15 = o_recv.at[0, pl.ds(0, 7)]
    rcopy(o15, o15, osend, orecv.at[0, 0], t, vx).wait_send()
    rcopy(o_recv.at[0], o_recv.at[0], osend, orecv.at[0, 0], t, vx).wait_send()
    s15 = t_recv.at[0, pl.ds(0, 7)]
    rcopy(s15, s15, ssend, srecv.at[0, 0], t, vx).wait_send()
    rcopy(t_recv.at[0], t_recv.at[0], ssend, srecv.at[0, 0], t, vx).wait_send()
    rcopy(d15, d15, dsend, drecv, t, vx).wait_send()
    rcopy(t15, t15, t2send, t2recv, t, vx).wait_send()

    @pl.when(c == 0)
    def _():
        rcopy(w_landed(15), w_landed(15), wzsend, wzrecv, t, vx).wait_send()

    @pl.when(c == 1)
    def _():
        rcopy(w_landed(16), w_landed(16), wzsend, wzrecv, t, vx).wait_send()


def on_device(
    text_rows, visual, norm_gain, q_weight, key_value_weight, q_gain, k_gain, out_weight, attn_gate
):
    vmem = pl.BlockSpec(memory_space=pltpu.VMEM)
    hbm = pl.BlockSpec(memory_space=pl.ANY)
    dma = pltpu.SemaphoreType.DMA
    one = dma(())
    buffers = [
        pltpu.VMEM(*buffer)
        for buffer in (
            ((32, 128), BF16),
            ((1, 128), F32),
            ((1, 128), F32),
            ((1, 128), F32),
            ((1, 1), F32),
            ((32, 128), BF16),
            ((2, 32, 2048), BF16),
            ((4096, 128), BF16),
            ((4096, 256), BF16),
            ((16, 256, 256), BF16),
            ((32, 128), BF16),
            ((16, 32, 128), BF16),
            ((2, 8, 2, 32, 128), BF16),
            ((2, 2, 128, 128), BF16),
            ((2, 512, 128), BF16),
            ((2, 8, 2, 32, 128), BF16),
            ((2, 8, 128), F32),
            ((2, 8, 2, 32, 128), BF16),
            ((2, 8, 8, 128), F32),
            ((16, 32, 128), BF16),
            ((16, 8, 128), F32),
            ((16, 32, 128), BF16),
            ((16, 8, 128), F32),
            ((32, 128), BF16),
            ((2, 32, 2048), BF16),
            ((2, 16, 128, 128), BF16),
        )
    ]
    semaphores = [
        dma((9,)),
        dma((30,)), dma((32,)),
        one, one,
        one, dma((2,)), one, one,
        one, dma((16,)), one, dma((2,)),
        dma((6,)), dma((6,)),
        one, dma((2, 8)), one, dma((2, 8)),
        one, one, one, one,
        one, dma((2,)), one, one,
        one, one, dma((7,)), dma((8,)), one, one,
    ]
    return pl.pallas_call(
        kernel,
        out_shape=jax.ShapeDtypeStruct((32, 128), BF16),
        in_specs=[hbm] * 9,
        out_specs=vmem,
        scratch_shapes=buffers + semaphores,
        compiler_params=pltpu.CompilerParams(
            collective_id=0, has_side_effects=True, vmem_limit_bytes=60 * 1024 * 1024
        ),
    )(
        text_rows, visual, norm_gain.reshape(1, -1), q_weight, key_value_weight,
        q_gain.reshape(1, -1), k_gain.reshape(1, -1), out_weight, attn_gate.reshape(1, 1),
    )


def solution(mesh):
    placed = (
        P("text", "vis"),
        P("vis", "text"),
        P(),
        P(None, "vis"),
        P(None, "text"),
        P(),
        P(),
        P("vis", None),
        P(),
    )
    return jax.shard_map(
        on_device, mesh=mesh, in_specs=placed, out_specs=P("text", "vis"), check_vma=False
    )
```

time: 86.8 us -> 85.6 us (0.986)
  the two profiles are of different devices: /device:TPU:16 before, /device:TPU:2 now
where the time goes in v3:
time: 85.6 us; the launch traced here: 85.3 us
  Pallas kernels  83.4 us (97%)
  local copies, waits for them, and re-layouts  1.3 us (2%)
    pallas_call x1, Pallas kernels, on_device(): pl.pallas_call(kernel, out_shape=jax.ShapeDtypeStruct((32, 128), BF16), i...  83.4 us

profile of v3, /device:TPU:2, one launch (start us, length us, event | category | flops | bytes accessed | tf_op | source)
XLA Modules:
  0.0 85.3 jit_solution(2072634706625361653)
XLA Ops:
  0.7 83.4 %shard_map.91 = bf16[32,128]{1,0:T(8,128)(2,1)} custom-call(bf16[32,128]{1,0:T(8,128)(2,1)} %text_hbm.1, bf16[512,256]{1,0:T(8,128)(2,1)} %vis_ref.1, f32[1,4096]{1,0:T(1,128)} %bitcast.5, bf16[4096,128]{1,0:T(8,128)(2,1)} %wq_hbm.1, bf16[4096,128]{1,0:T(8,128)(2,1)} %wkv_hbm.1, f32[1,128]{1,0:T(1,128)} %bitcast.6, f32[1,128]{1,0:T(1,128)} %bitcast.7, ...), custom_call_target="tpu_custom_call" | custom-call | tf_op jit(solution)/shard_map/pallas_call | solution.py:558
  84.1 1.3 %copy.12 = bf16[32,128]{1,0:T(8,128)(2,1)} copy(bf16[32,128]{1,0:T(8,128)(2,1)} %shard_map.91) | data formatting | bytes 16384

commit v4 on v3

--- a/solution.py
+++ b/solution.py
@@ -38,7 +38,7 @@
     out_ref,
     text_ref, gain_ref, qg_ref, kg_ref, gate_ref,
     text_s, text_all, wq, wk, vb, q_loc, q_heads, qbuf, kvst, kvb,
-    o_send, t_send, o_recv, t_recv, o2, t2, d_all, t_all, att, att_all, wo_all,
+    o_send, t_send, o_recv, t_recv, o2, t2, d_all, t_all, att, att_all, wo_all, terms_send, terms_recv,
     loc, vsend, vrecv, wsend, wrecv, tsend, trecv, txsend, txrecv,
     qzsend, qzrecv, qsend, qrecv, kvsend, kvrecv, osend, orecv, ssend, srecv,
     dsend, drecv, t2send, t2recv, asend, arecv, axsend, axrecv,
@@ -76,8 +76,29 @@
 
         lax.fori_loop(0, 15, step, 0)
 
+    def nearest(i):
+        bits = [(g // n % 2 + i // n % 2) % 2 for n in (1, 2, 4)]
+        return bits[0] + 2 * bits[1] + 4 * bits[2]
+
     def lanes(i):
         return pl.ds(pl.multiple_of(i * 128, 128), 128)
+
+    barrier = pltpu.get_barrier_semaphore()
+
+    def greet(tt, vv):
+        pl.semaphore_signal(barrier, inc=1, device_id=(tt, vv), device_id_type=MESH)
+
+    def greet_group(i, carry):
+        other = group + lax.rem(g + i, 8)
+        greet(other, v)
+        greet(other, vx)
+        return carry
+
+    each_z(lambda zz, i: greet(t, at_z(zz)))
+    for other in (far, far_sib, cross):
+        greet(other, v)
+    lax.fori_loop(1, 8, greet_group, 0)
+    greet(t, vx)
 
     small = [
         pltpu.make_async_copy(text_hbm, text_ref, loc.at[4]),
@@ -95,53 +116,31 @@
     own_wk.start()
     own_wq.start()
 
-    barrier = pltpu.get_barrier_semaphore()
-
-    def greet(tt, vv):
-        pl.semaphore_signal(barrier, inc=1, device_id=(tt, vv), device_id_type=MESH)
-
-    def greet_group(i, carry):
-        other = group + lax.rem(g + i, 8)
-        greet(other, v)
-        greet(other, vx)
-        return carry
-
-    for other in (far, far_sib, cross):
-        greet(other, v)
-    greet(t, vx)
-    lax.fori_loop(1, 8, greet_group, 0)
-    each_z(lambda zz, i: greet(t, at_z(zz)))
-
-    @pl.when(c == 1)
-    def _():
-        each_z(lambda zz, i: greet(t, 2 * zz + 1 - xl))
-
     for copy in small:
         copy.wait()
     text_s[...] = (text_ref[...].astype(F32) * gain_ref[...]).astype(BF16)
     text_all[xl, :, lanes(z)] = text_s[...]
-    pl.semaphore_wait(barrier, 3 + 1 + 14 + 15 + 15 * c)
-
-    def push_columns(block, everything, send, recv):
-        def push(zz, i):
-            near = jnp.where(i < 7, 1, 0)
-            rcopy(block, everything.at[xl, :, lanes(z)], send, recv.at[near], t, at_z(zz)).start()
-
-        each_z(push)
-
-    def forward_columns(everything, recv, xsend, xrecv, far_group):
-        count = 7 if far_group else 8
-        part = everything.at[0, :, pl.ds(0, count * 128)]
-        rcopy(part, part, xsend, recv.at[far_group], t, vx).wait_recv()
+    pl.semaphore_wait(barrier, 15 + 3 + 14 + 1)
+
+    groups = ((10, 23),), ((7, 10),)
+
+    def push_text(zz, i):
+        stage = jnp.where(i < 3, 1, 0)
+        rcopy(text_s, text_all.at[xl, :, lanes(z)], tsend, trecv.at[stage], t, at_z(zz)).start()
+
+    each_z(push_text)
+
+    def forward_text(stage):
+        part = text_all.at[0, :, pl.ds(0, (12, 3)[stage] * 128)]
+        rcopy(part, part, txsend, trecv.at[stage], t, vx).wait_recv()
 
         def forward(i, carry):
-            mine = everything.at[xl, :, lanes(lax.rem(z + i, 16))]
-            rcopy(mine, mine, xsend, xrecv, t, vx).start()
+            mine = text_all.at[xl, :, lanes(lax.rem(z + i, 16))]
+            rcopy(mine, mine, txsend, txrecv, t, vx).start()
             return carry
 
-        lax.fori_loop(*((5, 12) if far_group else (12, 21)), forward, 0)
-
-    push_columns(text_s, text_all, tsend, trecv)
+        for first, last in groups[stage]:
+            lax.fori_loop(first, last, forward, 0)
 
     sends = []
 
@@ -192,10 +191,10 @@
         relay(pdn0, h, up)
         relay(pup1, h, dn)
 
-    forward_columns(text_all, trecv, txsend, txrecv, 0)
     relays_first(0)
-    forward_columns(text_all, trecv, txsend, txrecv, 1)
-    relays_second(0)
+    forward_text(0)
+    relays_first(1)
+    forward_text(1)
 
     text_other = text_all.at[1 - xl]
     rcopy(text_other, text_other, txsend, txrecv, t, vx).wait_recv()
@@ -215,29 +214,19 @@
     )
 
     w_rows = pl.ds(pl.multiple_of((t // 2) * 16, 16), 16)
-    qw = (xl + c) % 2
-
-    def push_w(zz):
-        rcopy(
-            wo_hbm.at[w_rows, lanes(2 * zz + qw)], wo_all.at[xl, z, w_rows, :],
-            wzsend, wzrecv, t, 2 * zz + qw,
+    own_w = pltpu.make_async_copy(
+        wo_hbm.at[w_rows, lanes(2 * z + c)], wo_all.at[c, z, w_rows, :], loc.at[3]
+    )
+    own_w.start()
+    each_z(
+        lambda zz, i: rcopy(
+            wo_hbm.at[w_rows, lanes(2 * zz + c)], wo_all.at[c, z, w_rows, :],
+            wzsend, wzrecv, t, at_z(zz),
         ).start()
-
-    own_w = pltpu.make_async_copy(
-        wo_hbm.at[w_rows, lanes(v)], wo_all.at[xl, z, w_rows, :], loc.at[3]
-    )
-    each_z(lambda zz, i: push_w(zz))
-
-    @pl.when(c == 0)
-    def _():
-        own_w.start()
-
-    @pl.when(c == 1)
-    def _():
-        push_w(z)
-
-    relays_first(1)
-    relays_second(1)
+    )
+
+    for h in range(2):
+        relays_second(h)
 
     def share_heads(i, carry):
         other = lax.rem(z // 2 + 8 + jnp.where(i % 2 == 0, -(i // 2), (i + 1) // 2), 8)
@@ -297,7 +286,7 @@
     project(1)
 
     def w_block(f):
-        return wo_all.at[qw, :, pl.ds(pl.multiple_of((f // 2) * 16, 16), 16), :]
+        return wo_all.at[c, :, pl.ds(pl.multiple_of((f // 2) * 16, 16), 16), :]
 
     w_sends = []
 
@@ -310,18 +299,9 @@
     def w_got(f):
         rcopy(w_block(f), w_block(f), wpsend.at[0], wprecv.at[f // 2], sib, v).wait_recv()
 
-    def w_landed(count):
-        return wo_all.at[qw, pl.ds(0, count), pl.ds(0, 16), :]
-
-    @pl.when(c == 0)
-    def _():
-        own_w.wait()
-        rcopy(w_landed(15), w_landed(15), wzsend, wzrecv, t, vx).wait_recv()
-
-    @pl.when(c == 1)
-    def _():
-        rcopy(w_landed(16), w_landed(16), wzsend, wzrecv, t, vx).wait_recv()
-
+    w_landed = wo_all.at[c, pl.ds(0, 15), pl.ds(0, 16), :]
+    own_w.wait()
+    rcopy(w_landed, w_landed, wzsend, wzrecv, t, vx).wait_recv()
     w_send(t, xp, up, dn)
 
     q7 = qbuf.at[xl, pl.ds(0, 7)]
@@ -358,11 +338,11 @@
         ).start()
 
     def send_other(i, carry):
-        send_partial(1 - xl, lax.rem(g + i, 8), vx)
+        send_partial(1 - xl, nearest(7 - i), vx)
         return carry
 
     def send_own(i, carry):
-        send_partial(xl, lax.rem(g + i, 8), v)
+        send_partial(xl, nearest(8 - i), v)
         return carry
 
     attend(1 - xl)
@@ -381,7 +361,7 @@
     sub = lax.broadcasted_iota(jnp.int32, (8, 128), 0)
 
     def merge(i, carry):
-        src = lax.rem(g + i, 8)
+        src = nearest(i)
         for x in range(2):
 
             @pl.when(jnp.logical_or(x != xl, src != g))
@@ -431,6 +411,21 @@
     w_got(far)
     w_send(far, xp)
 
+    for copy in (*sends, w_out, *kv_sends, *w_sends):
+        copy.wait_send()
+    z15 = att_all.at[:, pl.ds(0, 15 * 128)]
+    rcopy(z15, z15, tsend, trecv.at[0], t, vx).wait_send()
+    rcopy(text_all.at[0], text_all.at[0], txsend, txrecv, t, vx).wait_send()
+    q15 = q_heads.at[pl.ds(0, 15)]
+    rcopy(q15, q15, qzsend, qzrecv.at[0], t, vx).wait_send()
+    for blocks in (q7, q8):
+        rcopy(blocks, blocks, qsend, qrecv.at[xl], t, vx).wait_send()
+    rcopy(w_landed, w_landed, wzsend, wzrecv, t, vx).wait_send()
+    for blocks in (o_recv.at[0], o_recv.at[0, pl.ds(0, 7)]):
+        rcopy(blocks, blocks, osend, orecv.at[0, 0], t, vx).wait_send()
+    for blocks in (t_recv.at[0], t_recv.at[0, pl.ds(0, 7)]):
+        rcopy(blocks, blocks, ssend, srecv.at[0, 0], t, vx).wait_send()
+
     d15, t15 = d_all.at[pl.ds(0, 15)], t_all.at[pl.ds(0, 15), pl.ds(0, 1), :]
     rcopy(t15, t15, t2send, t2recv, t, vx).wait_recv()
     rcopy(d15, d15, dsend, drecv, t, vx).wait_recv()
@@ -454,55 +449,41 @@
             num[k] = num[k] + block[8 * k : 8 * k + 8] * column(w, k)
     attended = jnp.concatenate([num[k] / column(den, k) for k in range(4)], axis=0)
     att[...] = attended.astype(BF16)
-    att_all[xl, :, lanes(z)] = att[...]
-    push_columns(att, att_all, asend, arecv)
+    att_all[:, lanes(z)] = att[...]
+    each_z(
+        lambda zz, i: rcopy(att, att_all.at[:, lanes(z)], asend, arecv, t, at_z(zz)).start()
+    )
 
     for f in (up, pup0, pdn0, pfar0):
         w_got(f)
-    w_sib = rcopy(wo_all.at[qw], wo_all.at[qw], wssend, wsrecv, sib, v)
+    w_sib = rcopy(wo_all.at[c], wo_all.at[c], wssend, wsrecv, sib, v)
     w_sib.start()
 
-    forward_columns(att_all, arecv, axsend, axrecv, 0)
-    forward_columns(att_all, arecv, axsend, axrecv, 1)
-    rcopy(wo_all.at[1 - qw], wo_all.at[1 - qw], wssend, wsrecv, sib, v).wait_recv()
-    att_other = att_all.at[1 - xl]
-    rcopy(att_other, att_other, axsend, axrecv, t, vx).wait_recv()
-    summed = jnp.zeros((32, 128), F32)
-    for n in range(2):
+    rcopy(wo_all.at[1 - c], wo_all.at[1 - c], wssend, wsrecv, sib, v).wait_recv()
+
+    rcopy(z15, z15, asend, arecv, t, vx).wait_recv()
+
+    def project_out(parity):
+        terms = jnp.zeros((32, 128), F32)
         for k in range(8):
-            summed = summed + jnp.dot(
-                att_all[n, :, k * 256 : k * 256 + 256],
-                wo_all[n, 2 * k : 2 * k + 2].reshape(256, 128),
+            terms = terms + jnp.dot(
+                att_all[:, k * 256 : k * 256 + 256],
+                wo_all[parity, 2 * k : 2 * k + 2].reshape(256, 128),
                 preferred_element_type=F32,
             )
-    out_ref[...] = (jnp.tanh(gate_ref[...]) * summed).astype(BF16)
-
-    for copy in (*sends, w_out, *kv_sends, *w_sends, w_sib):
-        copy.wait_send()
-    for everything, send, xsend in ((text_all, tsend, txsend), (att_all, asend, axsend)):
-        block = everything.at[0, :, pl.ds(0, 15 * 128)]
-        rcopy(block, block, send, trecv.at[0], t, vx).wait_send()
-        rcopy(everything.at[0], everything.at[0], xsend, trecv.at[0], t, vx).wait_send()
-    q15 = q_heads.at[pl.ds(0, 15)]
-    rcopy(q15, q15, qzsend, qzrecv.at[0], t, vx).wait_send()
-    rcopy(q7, q7, qsend, qrecv.at[xl], t, vx).wait_send()
-    rcopy(q8, q8, qsend, qrecv.at[xl], t, vx).wait_send()
-    o15 = o_recv.at[0, pl.ds(0, 7)]
-    rcopy(o15, o15, osend, orecv.at[0, 0], t, vx).wait_send()
-    rcopy(o_recv.at[0], o_recv.at[0], osend, orecv.at[0, 0], t, vx).wait_send()
-    s15 = t_recv.at[0, pl.ds(0, 7)]
-    rcopy(s15, s15, ssend, srecv.at[0, 0], t, vx).wait_send()
-    rcopy(t_recv.at[0], t_recv.at[0], ssend, srecv.at[0, 0], t, vx).wait_send()
+        return terms
+
+    terms_send[...] = project_out(1 - xl)
+    terms_x = rcopy(terms_send, terms_recv, axsend, axrecv, t, vx)
+    terms_x.start()
+    mine = project_out(xl)
+    terms_x.wait_recv()
+    out_ref[...] = (jnp.tanh(gate_ref[...]) * (mine + terms_recv[...])).astype(BF16)
+    w_sib.wait_send()
+    rcopy(z15, z15, asend, arecv, t, vx).wait_send()
+    terms_x.wait_send()
     rcopy(d15, d15, dsend, drecv, t, vx).wait_send()
     rcopy(t15, t15, t2send, t2recv, t, vx).wait_send()
-
-    @pl.when(c == 0)
-    def _():
-        rcopy(w_landed(15), w_landed(15), wzsend, wzrecv, t, vx).wait_send()
-
-    @pl.when(c == 1)
-    def _():
-        rcopy(w_landed(16), w_landed(16), wzsend, wzrecv, t, vx).wait_send()
 
 
 def on_device(
@@ -539,8 +520,10 @@
             ((16, 32, 128), BF16),
             ((16, 8, 128), F32),
             ((32, 128), BF16),
-            ((2, 32, 2048), BF16),
+            ((32, 2048), BF16),
             ((2, 16, 128, 128), BF16),
+            ((32, 128), F32),
+            ((32, 128), F32),
         )
     ]
     semaphores = [
@@ -552,7 +535,7 @@
         dma((6,)), dma((6,)),
         one, dma((2, 8)), one, dma((2, 8)),
         one, one, one, one,
-        one, dma((2,)), one, one,
+        one, one, one, one,
         one, one, dma((7,)), dma((8,)), one, one,
     ]
     return pl.pallas_call(

time: 85.6 us -> 81.5 us (0.952)
  Pallas kernels: 83.4 us -> 79.3 us
    pallas_call x1, Pallas kernels: 83.4 us -> 79.3 us  [on_device(): pl.pallas_call(kernel, out_shape=jax.ShapeDtypeStruct((32, 128), BF16), i...]
where the time goes in v4:
time: 81.5 us; the launch traced here: 81.3 us
  Pallas kernels  79.3 us (97%)
  local copies, waits for them, and re-layouts  1.3 us (2%)
    pallas_call x1, Pallas kernels, on_device(): pl.pallas_call(kernel, out_shape=jax.ShapeDtypeStruct((32, 128), BF16), i...  79.3 us

profile of v4, /device:TPU:2, one launch (start us, length us, event | category | flops | bytes accessed | tf_op | source)
XLA Modules:
  0.0 81.3 jit_solution(3557600559648658862)
XLA Ops:
  0.7 79.3 %shard_map.91 = bf16[32,128]{1,0:T(8,128)(2,1)} custom-call(bf16[32,128]{1,0:T(8,128)(2,1)} %text_hbm.1, bf16[512,256]{1,0:T(8,128)(2,1)} %vis_ref.1, f32[1,4096]{1,0:T(1,128)} %bitcast.5, bf16[4096,128]{1,0:T(8,128)(2,1)} %wq_hbm.1, bf16[4096,128]{1,0:T(8,128)(2,1)} %wkv_hbm.1, f32[1,128]{1,0:T(1,128)} %bitcast.6, f32[1,128]{1,0:T(1,128)} %bitcast.7, ...), custom_call_target="tpu_custom_call" | custom-call | tf_op jit(solution)/shard_map/pallas_call | solution.py:541
  80.0 1.3 %copy.12 = bf16[32,128]{1,0:T(8,128)(2,1)} copy(bf16[32,128]{1,0:T(8,128)(2,1)} %shard_map.91) | data formatting | bytes 16384

commit v5 on v4

--- a/solution.py
+++ b/solution.py
@@ -229,7 +229,7 @@
         relays_second(h)
 
     def share_heads(i, carry):
-        other = lax.rem(z // 2 + 8 + jnp.where(i % 2 == 0, -(i // 2), (i + 1) // 2), 8)
+        other = lax.rem(z // 2 + 6 + 4 * (i // 4) + (g + i) % 4, 8)
         for e in range(2):
             zz = 2 * other + e
 
@@ -302,7 +302,6 @@
     w_landed = wo_all.at[c, pl.ds(0, 15), pl.ds(0, 16), :]
     own_w.wait()
     rcopy(w_landed, w_landed, wzsend, wzrecv, t, vx).wait_recv()
-    w_send(t, xp, up, dn)
 
     q7 = qbuf.at[xl, pl.ds(0, 7)]
     rcopy(q7, q7, qsend, qrecv.at[xl], t, vx).wait_recv()
@@ -352,16 +351,13 @@
     o_recv[xl, g] = o_send[xl, g]
     t_recv[xl, g] = t_send[xl]
 
-    w_got(xp)
-    w_send(xp, up, dn)
-    w_got(dn)
-    w_send(dn, up)
+    w_send(t, xp, far, up, dn)
 
     lane = lax.broadcasted_iota(jnp.int32, (8, 128), 1)
     sub = lax.broadcasted_iota(jnp.int32, (8, 128), 0)
 
     def merge(i, carry):
-        src = nearest(i)
+        src = lax.rem(z // 2 + 8 + jnp.where(i % 2 == 0, -(i // 2), (i + 1) // 2) + 4, 8)
         for x in range(2):
 
             @pl.when(jnp.logical_or(x != xl, src != g))
@@ -408,8 +404,8 @@
 
     lax.fori_loop(0, 8, merge, 0)
 
-    w_got(far)
-    w_send(far, xp)
+    w_got(xp)
+    w_send(xp, far, up, dn)
 
     for copy in (*sends, w_out, *kv_sends, *w_sends):
         copy.wait_send()
@@ -454,7 +450,7 @@
         lambda zz, i: rcopy(att, att_all.at[:, lanes(z)], asend, arecv, t, at_z(zz)).start()
     )
 
-    for f in (up, pup0, pdn0, pfar0):
+    for f in (up, dn, far, pup0, pdn0, pfar0):
         w_got(f)
     w_sib = rcopy(wo_all.at[c], wo_all.at[c], wssend, wsrecv, sib, v)
     w_sib.start()

time: 81.5 us -> 75.1 us (0.921)
  Pallas kernels: 79.3 us -> 72.9 us
    pallas_call x1, Pallas kernels: 79.3 us -> 72.9 us  [on_device(): pl.pallas_call(kernel, out_shape=jax.ShapeDtypeStruct((32, 128), BF16), i...]
where the time goes in v5:
time: 75.1 us; the launch traced here: 74.9 us
  Pallas kernels  72.9 us (97%)
  local copies, waits for them, and re-layouts  1.3 us (2%)
    pallas_call x1, Pallas kernels, on_device(): pl.pallas_call(kernel, out_shape=jax.ShapeDtypeStruct((32, 128), BF16), i...  72.9 us

profile of v5, /device:TPU:2, one launch (start us, length us, event | category | flops | bytes accessed | tf_op | source)
XLA Modules:
  0.0 74.9 jit_solution(17792010376769736188)
XLA Ops:
  0.7 72.9 %shard_map.91 = bf16[32,128]{1,0:T(8,128)(2,1)} custom-call(bf16[32,128]{1,0:T(8,128)(2,1)} %text_hbm.1, bf16[512,256]{1,0:T(8,128)(2,1)} %vis_ref.1, f32[1,4096]{1,0:T(1,128)} %bitcast.5, bf16[4096,128]{1,0:T(8,128)(2,1)} %wq_hbm.1, bf16[4096,128]{1,0:T(8,128)(2,1)} %wkv_hbm.1, f32[1,128]{1,0:T(1,128)} %bitcast.6, f32[1,128]{1,0:T(1,128)} %bitcast.7, ...), custom_call_target="tpu_custom_call" | custom-call | tf_op jit(solution)/shard_map/pallas_call | solution.py:537
  73.6 1.3 %copy.12 = bf16[32,128]{1,0:T(8,128)(2,1)} copy(bf16[32,128]{1,0:T(8,128)(2,1)} %shard_map.91) | data formatting | bytes 16384

commit v6 on v5

--- a/solution.py
+++ b/solution.py
@@ -196,15 +196,22 @@
     relays_first(1)
     forward_text(1)
 
+    def project_text(q, parity):
+        for k in range(8):
+            weights = [
+                wq[pl.ds(pl.multiple_of((4 * k + 2 * e + parity) * 128, 128), 128), :] for e in range(2)
+            ]
+            q = q + jnp.dot(
+                text_all[parity, :, k * 256 : k * 256 + 256], jnp.concatenate(weights, axis=0),
+                preferred_element_type=F32,
+            )
+        return q
+
+    own_wq.wait()
+    q = project_text(jnp.zeros((32, 128), F32), xl)
     text_other = text_all.at[1 - xl]
     rcopy(text_other, text_other, txsend, txrecv, t, vx).wait_recv()
-    own_wq.wait()
-    q = jnp.zeros((32, 128), F32)
-    for k in range(16):
-        lhs = jnp.concatenate(
-            [text_all[0, :, k * 128 : k * 128 + 128], text_all[1, :, k * 128 : k * 128 + 128]], axis=1
-        )
-        q = q + jnp.dot(lhs, wq[k * 256 : k * 256 + 256, :], preferred_element_type=F32)
+    q = project_text(q, 1 - xl)
     q_loc[...] = head_norm(q, qg_ref[...]).astype(BF16)
     q_heads[z] = q_loc[...]
     each_z(
@@ -229,7 +236,8 @@
         relays_second(h)
 
     def share_heads(i, carry):
-        other = lax.rem(z // 2 + 6 + 4 * (i // 4) + (g + i) % 4, 8)
+        place = (g + i) % 2
+        other = lax.rem(z // 2 + 8 + jnp.where(place == 0, -(i // 2), i // 2 + 1), 8)
         for e in range(2):
             zz = 2 * other + e
 

time: 75.1 us -> 74.7 us (level)
  no operation moved by 1% of the time
where the time goes in v6:
time: 74.7 us; the launch traced here: 74.4 us
  Pallas kernels  72.5 us (97%)
  local copies, waits for them, and re-layouts  1.3 us (2%)
    pallas_call x1, Pallas kernels, on_device(): pl.pallas_call(kernel, out_shape=jax.ShapeDtypeStruct((32, 128), BF16), i...  72.5 us

profile of v6, /device:TPU:2, one launch (start us, length us, event | category | flops | bytes accessed | tf_op | source)
XLA Modules:
  0.0 74.4 jit_solution(18336514222348633541)
XLA Ops:
  0.7 72.5 %shard_map.91 = bf16[32,128]{1,0:T(8,128)(2,1)} custom-call(bf16[32,128]{1,0:T(8,128)(2,1)} %text_hbm.1, bf16[512,256]{1,0:T(8,128)(2,1)} %vis_ref.1, f32[1,4096]{1,0:T(1,128)} %bitcast.5, bf16[4096,128]{1,0:T(8,128)(2,1)} %wq_hbm.1, bf16[4096,128]{1,0:T(8,128)(2,1)} %wkv_hbm.1, f32[1,128]{1,0:T(1,128)} %bitcast.6, f32[1,128]{1,0:T(1,128)} %bitcast.7, ...), custom_call_target="tpu_custom_call" | custom-call | tf_op jit(solution)/shard_map/pallas_call | solution.py:545
  73.1 1.3 %copy.12 = bf16[32,128]{1,0:T(8,128)(2,1)} copy(bf16[32,128]{1,0:T(8,128)(2,1)} %shard_map.91) | data formatting | bytes 16384

commit v7 on v6

--- a/solution.py
+++ b/solution.py
@@ -165,12 +165,12 @@
 
     for h in range(2):
         send_block(t, h, sib, vis_ref.at[pl.ds((1 - c) * 256 + h * 128, 128), :])
-        for target in (up, dn, xp):
+        for target in (xp, up, dn):
             send_block(t, h, target, vis_ref.at[pl.ds(c * 256 + h * 128, 128), :])
     w_out = rcopy(wkv_hbm, wk.at[:, lanes(c)], wsend, wrecv, sib, v)
     w_out.start()
     for h in range(2):
-        relay(sib, h, up, dn, xp)
+        relay(sib, h, xp, up, dn)
 
     up0, up1 = (col + 4) % 16, (col + 5) % 16
     dn0, dn1 = (col + 12) % 16, (col + 13) % 16

time: 74.7 us -> 74.9 us (level)
  the two profiles are of different devices: /device:TPU:2 before, /device:TPU:34 now
where the time goes in v7:
time: 74.9 us; the launch traced here: 74.7 us
  Pallas kernels  72.7 us (97%)
  local copies, waits for them, and re-layouts  1.3 us (2%)
    pallas_call x1, Pallas kernels, on_device(): pl.pallas_call(kernel, out_shape=jax.ShapeDtypeStruct((32, 128), BF16), i...  72.7 us

profile of v7, /device:TPU:34, one launch (start us, length us, event | category | flops | bytes accessed | tf_op | source)
XLA Modules:
  0.0 74.7 jit_solution(9048141282632848193)
XLA Ops:
  0.7 72.7 %shard_map.91 = bf16[32,128]{1,0:T(8,128)(2,1)} custom-call(bf16[32,128]{1,0:T(8,128)(2,1)} %text_hbm.1, bf16[512,256]{1,0:T(8,128)(2,1)} %vis_ref.1, f32[1,4096]{1,0:T(1,128)} %bitcast.5, bf16[4096,128]{1,0:T(8,128)(2,1)} %wq_hbm.1, bf16[4096,128]{1,0:T(8,128)(2,1)} %wkv_hbm.1, f32[1,128]{1,0:T(1,128)} %bitcast.6, f32[1,128]{1,0:T(1,128)} %bitcast.7, ...), custom_call_target="tpu_custom_call" | custom-call | tf_op jit(solution)/shard_map/pallas_call | solution.py:545
  73.4 1.3 %copy.12 = bf16[32,128]{1,0:T(8,128)(2,1)} copy(bf16[32,128]{1,0:T(8,128)(2,1)} %shard_map.91) | data formatting | bytes 16384
